TPU v7x, 32 devices: a whole 2x2x4 slice. The times are simulated.
32 devices in a mesh: dp: 8 (over y, x, core), seq: 4 (over z).
Axes of the slice: x: 2, y: 2, z: 4, core: 2. Of those that a mesh axis runs over, the one named last changes fastest.
Arguments:
- hidden_in: bfloat16 [8, 2048, 2048], P('dp', 'seq'), may hold values from -6 to 6
- positions: int32 [8, 2048], P('dp', 'seq'), may hold values from 0 to 6141, as said below
- cotangent: bfloat16 [8, 2048, 2048], P('dp', 'seq'), may hold values from -6 to 6
- input_projection: float32 [2048, 4096], P(('dp', 'seq')), may hold values from -0.125 to 0.125
- out_proj: float32 [2048, 2048], P(('dp', 'seq')), may hold values from -1 to 1
- gate_up: float32 [2048, 12288], P(('dp', 'seq')), may hold values from -0.125 to 0.125
- down_proj: float32 [2048, 6144], P(('dp', 'seq')), may hold values from -0.078125 to 0.078125
- gains: float32 [4352], P(('dp', 'seq')), may hold values from 0.5 to 1.5
- input_first_moment: float32 [2048, 4096], P(('dp', 'seq')), may hold values from -32 to 32
- input_second_moment: float32 [2048, 4096], P(('dp', 'seq')), may hold values from 137.6256 to 557.056
- out_first: float32 [2048, 2048], P(('dp', 'seq')), may hold values from -6 to 6
- out_second: float32 [2048, 2048], P(('dp', 'seq')), may hold values from 4.25984 to 16.384
- gate_first: float32 [2048, 12288], P(('dp', 'seq')), may hold values from -32 to 32
- gate_second: float32 [2048, 12288], P(('dp', 'seq')), may hold values from 104.8576 to 425.984
- down_first: float32 [2048, 6144], P(('dp', 'seq')), may hold values from -48 to 48
- down_second: float32 [2048, 6144], P(('dp', 'seq')), may hold values from 311.296 to 1245.184
- gain_first: float32 [4352], P(('dp', 'seq')), may hold values from -64 to 64
- gain_second: float32 [4352], P(('dp', 'seq')), may hold values from 557.056 to 2211.84
Outputs:
- layer_out: bfloat16 [8, 2048, 2048], P('dp', 'seq')
- input_grad: float32 [8, 2048, 2048], P('dp', 'seq')
- in_proj_new: float32 [2048, 4096], P(('dp', 'seq'))
- in_first_new: float32 [2048, 4096], P(('dp', 'seq'))
- in_second_new: float32 [2048, 4096], P(('dp', 'seq'))
- out_proj_new: float32 [2048, 2048], P(('dp', 'seq'))
- out_first_new: float32 [2048, 2048], P(('dp', 'seq'))
- out_second_new: float32 [2048, 2048], P(('dp', 'seq'))
- gate_up_new: float32 [2048, 12288], P(('dp', 'seq'))
- gate_first_new: float32 [2048, 12288], P(('dp', 'seq'))
- gate_second_new: float32 [2048, 12288], P(('dp', 'seq'))
- down_proj_new: float32 [2048, 6144], P(('dp', 'seq'))
- down_first_new: float32 [2048, 6144], P(('dp', 'seq'))
- down_second_new: float32 [2048, 6144], P(('dp', 'seq'))
- gains_new: float32 [4352], P(('dp', 'seq'))
- gain_first_new: float32 [4352], P(('dp', 'seq'))
- gain_second_new: float32 [4352], P(('dp', 'seq'))
Inputs may be any that keep to these rules, and one draw needn't show every extreme that they name: Within each sequence, positions start at 0 and rise by 1 to 3 from one token to the next.
All inputs are finite; a program needn't handle non-finite values.
Results may differ from a plain program's by a relative error of at most 0.014.
The roundings to bfloat16 on the way count: a program that leaves them out, or rounds other values in their place, can miss the bound.
Values may be sent and summed in bfloat16 or wider, within the bound.
No kernel may reach another device: no remote copies, remote signals or barrier semaphores. Data moves between devices by JAX's collectives and lax.ppermute only.
A program may use at most 512 MiB of HBM per device.

v0:
```python
import math

import jax
import jax.numpy as jnp
from jax import lax
from jax.sharding import PartitionSpec as P

MODEL_WIDTH = 2048
QUERY_HEADS = 16
KEY_VALUE_HEADS = 8
HEAD_SIZE = 128
FF = 6144
STEP = 10


norm_eps = 1e-06
rope_base = 1000000.0
beta_one = 0.9
beta_two = 0.95
adam_eps = 1e-08
weight_decay = 0.1
masked_score = -1e30


def rms_scale(values):
    return lax.rsqrt(jnp.mean(values * values, axis=-1, keepdims=True) + norm_eps)


def norm_back(scaling, normed, upstream):
    return scaling * (upstream - normed * jnp.mean(upstream * normed, axis=-1, keepdims=True))


def rotary_tables(places, extent):
    half_dim = extent // 2
    freqs = jnp.exp(jnp.arange(half_dim, dtype=jnp.float32) * (-2.0 * math.log(rope_base) / extent))
    angles = places.astype(jnp.float32)[:, None] * freqs[None, :]
    return (jnp.cos(angles), jnp.sin(angles))


def rotate(values, cosine_table, sine_table):
    half_dim = values.shape[-1] // 2
    first_half = values[..., :half_dim]
    second_half = values[..., half_dim:]
    cos_wide = cosine_table[:, None, :]
    sin_wide = sine_table[:, None, :]
    return jnp.concatenate(
        [
            first_half * cos_wide - second_half * sin_wide,
            second_half * cos_wide + first_half * sin_wide,
        ],
        axis=-1,
    )


def rotate_back(values, cosine_table, sine_table):
    half_dim = values.shape[-1] // 2
    first_half = values[..., :half_dim]
    second_half = values[..., half_dim:]
    cos_wide = cosine_table[:, None, :]
    sin_wide = sine_table[:, None, :]
    return jnp.concatenate(
        [
            first_half * cos_wide + second_half * sin_wide,
            second_half * cos_wide - first_half * sin_wide,
        ],
        axis=-1,
    )


def contract_rows(left, right):
    return lax.dot_general(
        left, right, (((0,), (0,)), ((), ())), preferred_element_type=jnp.float32
    )


def times_transposed(left, right):
    return lax.dot_general(
        left, right, (((1,), (1,)), ((), ())), preferred_element_type=jnp.float32
    )


def split_gains(gathered):
    gain_all = gathered.astype(jnp.float32)
    return (
        gain_all[:MODEL_WIDTH],
        gain_all[MODEL_WIDTH : 2 * MODEL_WIDTH],
        gain_all[2 * MODEL_WIDTH : 2 * MODEL_WIDTH + HEAD_SIZE],
        gain_all[2 * MODEL_WIDTH + HEAD_SIZE :],
    )


def block_scores(grouped, keys, offset, block_rows, scaling):
    sequence_length = keys.shape[0]
    query_block = lax.dynamic_slice_in_dim(grouped, offset, block_rows, 0)
    scores = (
        jnp.einsum("qgrd,kgd->grqk", query_block, keys, preferred_element_type=jnp.float32)
        * scaling
    )
    causal = (offset + jnp.arange(block_rows, dtype=jnp.int32))[:, None] >= jnp.arange(
        sequence_length, dtype=jnp.int32
    )[None, :]
    return (query_block, causal, jnp.where(causal, scores, masked_score))


def attend(queries, keys, values):
    sequence_length, local_heads, head_dim = queries.shape
    kv_local = keys.shape[1]
    grouped = queries.reshape(sequence_length, kv_local, local_heads // kv_local, head_dim)
    block_rows = min(512, sequence_length)
    block_count = sequence_length // block_rows
    scaling = head_dim ** (-0.5)

    def one_block(index):
        query_block, causal, scores = block_scores(
            grouped, keys, index * block_rows, block_rows, scaling
        )
        highest = jnp.max(scores, axis=-1, keepdims=True)
        expd = jnp.exp(scores - highest)
        totals = jnp.sum(expd, axis=-1, keepdims=True)
        weights = (expd / totals).astype(jnp.bfloat16)
        result = jnp.einsum("grqk,kgd->qgrd", weights, values, preferred_element_type=jnp.float32)
        return (result, highest[..., 0] + jnp.log(totals[..., 0]))

    blocks, log_sums = lax.map(one_block, jnp.arange(block_count, dtype=jnp.int32))
    return (blocks.reshape(sequence_length, local_heads, head_dim), log_sums)


def attend_back(queries, keys, values, upstream, log_sums):
    sequence_length, local_heads, head_dim = queries.shape
    kv_local = keys.shape[1]
    head_repeat_count = local_heads // kv_local
    grouped = queries.reshape(sequence_length, kv_local, head_repeat_count, head_dim)
    up_grouped = upstream.reshape(sequence_length, kv_local, head_repeat_count, head_dim)
    block_rows = min(512, sequence_length)
    block_count = sequence_length // block_rows
    scaling = head_dim ** (-0.5)

    def one_block(carry, index):
        key_acc, value_acc = carry
        offset = index * block_rows
        query_block, causal, scores = block_scores(grouped, keys, offset, block_rows, scaling)
        up_block = lax.dynamic_slice_in_dim(up_grouped, offset, block_rows, 0)
        probs = jnp.where(causal, jnp.exp(scores - log_sums[index][..., None]), 0.0)
        grad_probs = jnp.einsum(
            "qgrd,kgd->grqk", up_block, values, preferred_element_type=jnp.float32
        )
        inner = jnp.sum(grad_probs * probs, axis=-1, keepdims=True)
        grad_scores = (probs * (grad_probs - inner)).astype(jnp.bfloat16)
        grad_query = (
            jnp.einsum("grqk,kgd->qgrd", grad_scores, keys, preferred_element_type=jnp.float32)
            * scaling
        )
        key_acc = (
            key_acc
            + jnp.einsum(
                "grqk,qgrd->kgd", grad_scores, query_block, preferred_element_type=jnp.float32
            )
            * scaling
        )
        value_acc = value_acc + jnp.einsum(
            "grqk,qgrd->kgd",
            probs.astype(jnp.bfloat16),
            up_block,
            preferred_element_type=jnp.float32,
        )
        return ((key_acc, value_acc), grad_query)

    zeros = jnp.zeros((sequence_length, kv_local, head_dim), jnp.float32)
    (key_grad, value_grad), query_grad = lax.scan(
        one_block, (zeros, zeros), jnp.arange(block_count, dtype=jnp.int32)
    )
    return (query_grad.reshape(sequence_length, local_heads, head_dim), key_grad, value_grad)


def adamw_update(param, gradient, first, second, rate, decay):
    first = beta_one * first + (1.0 - beta_one) * gradient
    second = beta_two * second + (1.0 - beta_two) * gradient * gradient
    first_hat = first / (1.0 - beta_one**STEP)
    second_hat = second / (1.0 - beta_two**STEP)
    param = param - rate * (first_hat / (jnp.sqrt(second_hat) + adam_eps) + decay * param)
    return (param, first, second)


def gather_whole(in_part, out_part, gate_part, down_part, gain_part):
    return (
        lax.all_gather(in_part, ("dp", "seq"), axis=0, tiled=True),
        lax.all_gather(out_part, ("dp", "seq"), axis=0, tiled=True),
        lax.all_gather(gate_part, ("dp", "seq"), axis=0, tiled=True),
        lax.all_gather(down_part, ("dp", "seq"), axis=0, tiled=True),
        lax.all_gather(gain_part, ("dp", "seq"), axis=0, tiled=True),
    )


def whole_plan(
    hidden_in, positions, cotangent, input_projection, out_proj, gate_up, down_proj, gains
):
    sequence_count, local_length, model_dim = hidden_in.shape
    count_of_rows = sequence_count * local_length
    query_width = QUERY_HEADS * HEAD_SIZE
    key_width = KEY_VALUE_HEADS * HEAD_SIZE
    in_cast = input_projection.astype(jnp.bfloat16)
    out_cast = out_proj.astype(jnp.bfloat16)
    gate_cast = gate_up.astype(jnp.bfloat16)
    down_cast = down_proj.astype(jnp.bfloat16)
    gains_cast = gains.astype(jnp.bfloat16)
    in_low, out_low, gate_low, down_low, gains_low = gather_whole(
        in_cast, out_cast, gate_cast, down_cast, gains_cast
    )
    gain_attn, gain_mlp, gain_query, gain_key = split_gains(gains_low)
    inputs = hidden_in.astype(jnp.float32).reshape(count_of_rows, model_dim)
    first_scale = rms_scale(inputs)
    first_normed = inputs * first_scale
    attn_in = (first_normed * gain_attn).astype(jnp.bfloat16)
    projected_rows = jnp.dot(attn_in, in_low, preferred_element_type=jnp.float32)
    query_raw = projected_rows[:, :query_width].reshape(count_of_rows, QUERY_HEADS, HEAD_SIZE)
    key_unrotated = projected_rows[:, query_width : query_width + key_width].reshape(
        count_of_rows, KEY_VALUE_HEADS, HEAD_SIZE
    )
    value_per_head = projected_rows[:, query_width + key_width :].astype(jnp.bfloat16)
    cosine_table, sine_table = rotary_tables(positions.reshape(count_of_rows), HEAD_SIZE)
    query_scale = rms_scale(query_raw)
    query_norm = query_raw * query_scale
    query_rot = rotate(query_norm * gain_query, cosine_table, sine_table).astype(jnp.bfloat16)
    key_scale = rms_scale(key_unrotated)
    key_norm = key_unrotated * key_scale
    key_rotated = rotate(key_norm * gain_key, cosine_table, sine_table).astype(jnp.bfloat16)
    heads_query, heads_key, heads_value = (
        lax.all_to_all(
            query_rot.reshape(sequence_count, local_length, QUERY_HEADS, HEAD_SIZE),
            "seq",
            split_axis=2,
            concat_axis=1,
            tiled=True,
        ),
        lax.all_to_all(
            key_rotated.reshape(sequence_count, local_length, KEY_VALUE_HEADS, HEAD_SIZE),
            "seq",
            split_axis=2,
            concat_axis=1,
            tiled=True,
        ),
        lax.all_to_all(
            value_per_head.reshape(sequence_count, local_length, KEY_VALUE_HEADS, HEAD_SIZE),
            "seq",
            split_axis=2,
            concat_axis=1,
            tiled=True,
        ),
    )
    attended, log_sums = lax.map(
        lambda element: attend(*element), (heads_query, heads_key, heads_value)
    )
    returned = lax.all_to_all(
        attended.astype(jnp.bfloat16), "seq", split_axis=1, concat_axis=2, tiled=True
    )
    mixed_heads = returned.reshape(count_of_rows, query_width)
    attn_out = times_transposed(mixed_heads, out_low)
    residual = inputs + attn_out
    second_scale = rms_scale(residual)
    second_normed = residual * second_scale
    mlp_low = (second_normed * gain_mlp).astype(jnp.bfloat16)
    gate_up_raw = jnp.dot(mlp_low, gate_low, preferred_element_type=jnp.float32)
    gate_pre = gate_up_raw[:, :FF]
    up_pre = gate_up_raw[:, FF:]
    gate_sig = jax.nn.sigmoid(gate_pre)
    gate_act = gate_pre * gate_sig
    hidden = (gate_act * up_pre).astype(jnp.bfloat16)
    mlp_out = times_transposed(hidden, down_low)
    layer_out = (
        (residual + mlp_out).astype(jnp.bfloat16).reshape(sequence_count, local_length, model_dim)
    )
    in_low, out_low, gate_low, down_low, gains_low = gather_whole(
        in_cast, out_cast, gate_cast, down_cast, gains_cast
    )
    gain_attn, gain_mlp, gain_query, gain_key = split_gains(gains_low)
    upstream = cotangent.reshape(count_of_rows, model_dim)
    sum_down = contract_rows(upstream, hidden)
    grad_hidden = jnp.dot(upstream, down_low, preferred_element_type=jnp.float32)
    grad_gate = grad_hidden * up_pre * gate_sig * (1.0 + gate_pre * (1.0 - gate_sig))
    grad_up = grad_hidden * gate_act
    grad_gate_up = jnp.concatenate([grad_gate, grad_up], axis=1).astype(jnp.bfloat16)
    sum_gate_up = contract_rows(mlp_low, grad_gate_up)
    grad_mlp_in = times_transposed(grad_gate_up, gate_low)
    sum_g_mlp = jnp.sum(grad_mlp_in * second_normed, axis=0)
    grad_residual = upstream.astype(jnp.float32) + norm_back(
        second_scale, second_normed, grad_mlp_in * gain_mlp
    )
    mlp_sums = (
        lax.psum_scatter(sum_gate_up, ("dp", "seq"), scatter_dimension=0, tiled=True),
        lax.psum_scatter(sum_down, ("dp", "seq"), scatter_dimension=0, tiled=True),
    )
    grad_attn_out = grad_residual.astype(jnp.bfloat16)
    sum_out = contract_rows(grad_attn_out, mixed_heads)
    grad_attended = (
        jnp.dot(grad_attn_out, out_low, preferred_element_type=jnp.float32)
        .astype(jnp.bfloat16)
        .reshape(sequence_count, local_length, QUERY_HEADS, HEAD_SIZE)
    )
    grad_heads = lax.all_to_all(grad_attended, "seq", split_axis=2, concat_axis=1, tiled=True)
    grad_query_h, grad_key_h, grad_value_h = lax.map(
        lambda element: attend_back(*element),
        (heads_query, heads_key, heads_value, grad_heads, log_sums),
    )
    grad_query_s, grad_key_split, grad_value_s = (
        lax.all_to_all(
            grad_query_h.astype(jnp.bfloat16), "seq", split_axis=1, concat_axis=2, tiled=True
        ),
        lax.all_to_all(
            grad_key_h.astype(jnp.bfloat16), "seq", split_axis=1, concat_axis=2, tiled=True
        ),
        lax.all_to_all(
            grad_value_h.astype(jnp.bfloat16), "seq", split_axis=1, concat_axis=2, tiled=True
        ),
    )
    query_unrot = rotate_back(
        grad_query_s.reshape(count_of_rows, QUERY_HEADS, HEAD_SIZE).astype(jnp.float32),
        cosine_table,
        sine_table,
    )
    key_unrot = rotate_back(
        grad_key_split.reshape(count_of_rows, KEY_VALUE_HEADS, HEAD_SIZE).astype(jnp.float32),
        cosine_table,
        sine_table,
    )
    sum_g_query = jnp.sum(query_unrot * query_norm, axis=(0, 1))
    sum_g_key = jnp.sum(key_unrot * key_norm, axis=(0, 1))
    grad_query_raw = norm_back(query_scale, query_norm, query_unrot * gain_query)
    grad_key_raw = norm_back(key_scale, key_norm, key_unrot * gain_key)
    grad_projected = jnp.concatenate(
        [
            grad_query_raw.reshape(count_of_rows, query_width).astype(jnp.bfloat16),
            grad_key_raw.reshape(count_of_rows, key_width).astype(jnp.bfloat16),
            grad_value_s.reshape(count_of_rows, key_width),
        ],
        axis=1,
    )
    sum_in = contract_rows(attn_in, grad_projected)
    grad_attn_in = times_transposed(grad_projected, in_low)
    sum_g_attn = jnp.sum(grad_attn_in * first_normed, axis=0)
    input_grad = grad_residual + norm_back(first_scale, first_normed, grad_attn_in * gain_attn)
    sum_gains = jnp.concatenate([sum_g_attn, sum_g_mlp, sum_g_query, sum_g_key])
    attn_sums = (
        lax.psum_scatter(sum_in, ("dp", "seq"), scatter_dimension=0, tiled=True),
        lax.psum_scatter(sum_out, ("dp", "seq"), scatter_dimension=0, tiled=True),
        lax.psum_scatter(sum_gains, ("dp", "seq"), scatter_dimension=0, tiled=True),
    )
    return (
        layer_out,
        input_grad.reshape(sequence_count, local_length, model_dim),
        attn_sums[0],
        attn_sums[1],
        mlp_sums[0],
        mlp_sums[1],
        attn_sums[2],
    )


def per_device(
    hidden_in,
    positions,
    cotangent,
    input_projection,
    out_proj,
    gate_up,
    down_proj,
    gains,
    input_first_moment,
    input_second_moment,
    out_first,
    out_second,
    gate_first,
    gate_second,
    down_first,
    down_second,
    gain_first,
    gain_second,
):
    results = whole_plan(
        hidden_in, positions, cotangent, input_projection, out_proj, gate_up, down_proj, gains
    )
    layer_out, input_grad, in_grad, out_grad, gate_grad, down_grad, gain_grad = results
    in_new = adamw_update(
        input_projection,
        in_grad,
        input_first_moment,
        input_second_moment,
        1.0 / math.sqrt(MODEL_WIDTH),
        weight_decay,
    )
    out_new = adamw_update(
        out_proj,
        out_grad,
        out_first,
        out_second,
        8.0 / math.sqrt(QUERY_HEADS * HEAD_SIZE),
        weight_decay,
    )
    gate_new = adamw_update(
        gate_up, gate_grad, gate_first, gate_second, 1.0 / math.sqrt(MODEL_WIDTH), weight_decay
    )
    down_new = adamw_update(
        down_proj, down_grad, down_first, down_second, 1.0 / math.sqrt(FF), weight_decay
    )
    gain_new = adamw_update(gains, gain_grad, gain_first, gain_second, 0.5, 0.0)
    return (
        layer_out,
        input_grad,
        in_new[0],
        in_new[1],
        in_new[2],
        out_new[0],
        out_new[1],
        out_new[2],
        gate_new[0],
        gate_new[1],
        gate_new[2],
        down_new[0],
        down_new[1],
        down_new[2],
        gain_new[0],
        gain_new[1],
        gain_new[2],
    )


def solution(mesh):
    return jax.shard_map(
        per_device,
        mesh=mesh,
        in_specs=(
            P("dp", "seq", None),
            P("dp", "seq"),
            P("dp", "seq", None),
            P(("dp", "seq"), None),
            P(("dp", "seq"), None),
            P(("dp", "seq"), None),
            P(("dp", "seq"), None),
            P(("dp", "seq")),
            P(("dp", "seq"), None),
            P(("dp", "seq"), None),
            P(("dp", "seq"), None),
            P(("dp", "seq"), None),
            P(("dp", "seq"), None),
            P(("dp", "seq"), None),
            P(("dp", "seq"), None),
            P(("dp", "seq"), None),
            P(("dp", "seq")),
            P(("dp", "seq")),
        ),
        out_specs=(
            P("dp", "seq", None),
            P("dp", "seq", None),
            P(("dp", "seq"), None),
            P(("dp", "seq"), None),
            P(("dp", "seq"), None),
            P(("dp", "seq"), None),
            P(("dp", "seq"), None),
            P(("dp", "seq"), None),
            P(("dp", "seq"), None),
            P(("dp", "seq"), None),
            P(("dp", "seq"), None),
            P(("dp", "seq"), None),
            P(("dp", "seq"), None),
            P(("dp", "seq"), None),
            P(("dp", "seq")),
            P(("dp", "seq")),
            P(("dp", "seq")),
        ),
        check_vma=False,
    )
```

profile of v0, /device:TPU:0, one launch (start us, length us, event | category | flops | bytes accessed | tf_op | source)
XLA Modules:
  0.0 3303.5 jit_solution(16022227256647841653)
XLA Ops:
  15.7 43.5 %all-reduce = bf16[4352]{0:T(1024)(128)(2,1)S(1)} all-reduce(bf16[4352]{0:T(1024)(128)(2,1)S(1)} %dynamic-update-slice), channel_id=1, replica_groups=mesh['dp'=8,'seq'=4] {'dp','seq'}, use_global_device_ids=true, to_apply=%add | all-reduce | flops 4352 | bytes 17408
  61.3 68.7 %all-gather.5.cloned.1.call-done = bf16[2048,4096]{1,0:T(8,128)(2,1)} async-done(((bf16[64,4096]{1,0:T(8,128)(2,1)}), bf16[2048,4096]{1,0:T(8,128)(2,1)}) %all-gather.5.cloned.1.call-update) | async-done | bytes 16777232 | tf_op jit(solution)/shard_map/all_gather | solution.py:186
  155.6 34.4 %all-to-all-done.1 = bf16[1,512,8,128]{3,1,0,2:T(8,128)(2,1)S(1)} async-done(((bf16[1,512,8,128]{3,1,0,2:T(8,128)(2,1)}), bf16[1,512,8,128]{3,1,0,2:T(8,128)(2,1)S(1)}, u32[]{:S(2)}, u32[]{:S(2)}) %all-to-all-start.1) | async-done | bytes 1048608 | tf_op jit(solution)/shard_map/all_to_all | solution.py:235
  209.2 32.6 all-to-all-done.2
  249.0 79.5 %all-to-all-done = bf16[1,512,16,128]{3,1,0,2:T(8,128)(2,1)S(1)} async-done(((bf16[1,512,16,128]{3,1,0,2:T(8,128)(2,1)}), bf16[1,512,16,128]{3,1,0,2:T(8,128)(2,1)S(1)}, u32[]{:S(2)}, u32[]{:S(2)}) %all-to-all-start) | async-done | bytes 2097184 | tf_op jit(solution)/shard_map/all_to_all | solution.py:228
  333.4 72.7 %while.47 = (s32[]{:T(128)}, bf16[4,512,2,2,128]{4,1,0,3,2:T(8,128)(2,1)}, f32[4,2,2,512]{3,2,1,0:T(2,128)}, s32[4]{0:T(128)S(1)}, bf16[2048,2,2,128]{3,0,2,1:T(...) while((s32[]{:T(128)}, ...), condition=%wide.region_6.7_spmd, body=%wide.region_3.6_spmd.sunk | while | flops 2198862336 | bytes 58266800 | solution.py:124
  410.3 104.8 %all_to_all.108 = bf16[1,2048,4,128]{3,2,0,1:T(4,128)(2,1)S(1)} all-to-all(bf16[1,2048,4,128]{3,2,0,1:T(4,128)(2,1)S(1)} %copy.297), channel_id=1, replica_groups=mesh['dp'=8,'seq'=4] {'seq'}, dimensions={1} | all-to-all | bytes 4194304 | tf_op jit(solution)/shard_map/all_to_all | solution.py:253
  531.7 65.9 %all-gather.9.cloned.1.call-done = bf16[2048,12288]{1,0:T(8,128)(2,1)} async-done(((bf16[64,12288]{1,0:T(8,128)(2,1)}), bf16[2048,12288]{1,0:T(8,128)(2,1)}) %all-gather.9.cloned.1.call-update) | async-done | bytes 50331664 | tf_op jit(solution)/shard_map/all_gather | solution.py:188
  597.6 37.2 %fusion.96 = f32[512,12288]{1,0:T(8,128)} fusion(bf16[2048,12288]{1,0:T(8,128)(2,1)} %all-gather.9.cloned.1.call-done, f32[512,2048]{1,0:T(8,128)} %get-tuple-element.415, f32[2048]{0:T(1024)S(1)} %copy-done.25, f32[512]{0:T(512)S(1)} %add_rsqrt_fusion.2), kind=kOutput, calls=%fused_computation.186 | convolution fusion | flops 25772949504 | bytes 79702016 | tf_op jit(solution)/shard_map/dot_general | solution.py:262
  634.9 119.8 %all-gather.11.cloned.1.call-done = bf16[2048,6144]{1,0:T(8,128)(2,1)} async-done(((bf16[64,6144]{1,0:T(8,128)(2,1)}), bf16[2048,6144]{1,0:T(8,128)(2,1)}) %all-gather.11.cloned.1.call-update) | async-done | bytes 25165840 | tf_op jit(solution)/shard_map/all_gather | solution.py:189
  754.6 32.5 multiply_convert_fusion.1
  787.1 36.2 %multiply_reduce_fusion = (f32[2048]{0:T(1024)}, f32[512]{0:T(512)S(1)}, f32[512,2048]{1,0:T(8,128)}) fusion(f32[512,2048]{1,0:T(8,128)} %get-tuple-element.415, f32[512]{0:T(512)S(1)} %add_rsqrt_fusion.2, f32[2048]{0:T(1024)S(1)} %copy-done.25, bf16[2048,12288]{1,0:T(8,128)(2,1)} %all-gather.9.cloned.1.call-done, ...), kind=kOutput, calls=%fused_computation.90 | convolution fusion | flops 25801259008 | bytes 71323648 | tf_op jit(solution)/shard_map/dot_general | solution.py:77
  840.8 22.7 convolution_bitcast_fusion.1
  863.5 49.0 %copy.327 = f32[2048,6144]{1,0:T(8,128)} copy(f32[2048,6144]{0,1:T(8,128)} %convolution_bitcast_fusion.1) | data formatting | bytes 100663296
  928.7 103.2 %all-to-all-done.4 = bf16[1,512,16,128]{3,1,0,2:T(8,128)(2,1)} async-done(((bf16[1,512,16,128]{3,1,0,2:T(8,128)(2,1)}), bf16[1,512,16,128]{3,1,0,2:T(8,128)(2,1)}, u32[]{:S(2)}, u32[]{:S(2)}) %all-to-all-start.4) | async-done | bytes 2097184 | tf_op jit(solution)/shard_map/all_to_all | solution.py:299
  1036.8 251.3 %while.48 = (s32[]{:T(128)}, f32[2048,2,128]{0,2,1:T(8,128)S(1)}, f32[2048,2,128]{0,2,1:T(8,128)}, bf16[4,512,2,2,128]{4,1,0,3,2:T(8,128)(2,1)}, s32[4]{0:T(128)...) while((s32[]{:T(128)}, f32[2048,2,128]{0,2,1:T(8,128)S(1)}, ...), condition=%wide.region_11.12_spmd.clone, body=%wide.region_9.11_spmd.clone.sunk | while | flops 5414582784 | bytes 210809648 | solution.py:169
  1335.6 42.6 %all-to-all-done.7 = bf16[1,2048,2,128]{3,2,0,1:T(2,128)(2,1)} async-done(((bf16[1,2048,2,128]{3,2,0,1:T(2,128)(2,1)}), bf16[1,2048,2,128]{3,2,0,1:T(2,128)(2,1)}, u32[]{:S(2)}, u32[]{:S(2)}) %all-to-all-start.7) | async-done | bytes 1048608 | tf_op jit(solution)/shard_map/all_to_all | solution.py:311
  1400.2 78.0 %all-to-all-done.5 = bf16[1,2048,4,128]{3,2,0,1:T(4,128)(2,1)S(1)} async-done(((bf16[1,2048,4,128]{3,2,0,1:T(4,128)(2,1)}), bf16[1,2048,4,128]{3,2,0,1:T(4,128)(2,1)S(1)}, u32[]{:S(2)}, u32[]{:S(2)}) %all-to-all-start.5) | async-done | bytes 2097184 | tf_op jit(solution)/shard_map/all_to_all | solution.py:305
  1513.9 45.9 %fusion.43 = f32[2048,12288]{1,0:T(8,128)} fusion(bf16[512,6144]{1,0:T(8,128)(2,1)} %get-tuple-element.386, bf16[512,6144]{1,0:T(8,128)(2,1)} %get-tuple-element.385, f32[512,2048]{1,0:T(8,128)} %get-tuple-element.415, f32[2048]{0:T(1024)S(1)} %copy-done.26, f32[512]{0:T(512)S(1)} %copy-done.28), kind=kOutput, calls=%fused_computation.60 | convolution fusion | flops 25798115328 | bytes 117450752 | tf_op jit(solution)/shard_map/dot_general | solution.py:71
  1559.8 21.4 fusion.63
  1596.7 41.4 %all-reduce.1 = f32[4352]{0:T(1024)S(1)} all-reduce(f32[4352]{0:T(1024)S(1)} %pad_maximum_fusion.9), channel_id=6, replica_groups=mesh['dp'=8,'seq'=4] {'dp','seq'}, use_global_device_ids=true, to_apply=%region_25.26.clone | all-reduce | flops 4352 | bytes 34816
  1648.2 95.8 %reduce-scatter.13.cloned.1.call-done = f32[64,6144]{1,0:T(8,128)} async-done(((f32[2048,6144]{1,0:T(8,128)}), f32[64,6144]{1,0:T(8,128)}) %reduce-scatter.13.cloned.1.call-update) | async-done | bytes 1572880 | tf_op jit(solution)/shard_map/reduce_scatter | solution.py:290
  1749.2 707.9 %reduce-scatter.7.cloned.1.call-done = f32[64,4096]{1,0:T(8,128)} async-done(((f32[2048,4096]{1,0:T(8,128)}), f32[64,4096]{1,0:T(8,128)}) %reduce-scatter.7.cloned.1.call-update) | async-done | bytes 1048592 | tf_op jit(solution)/shard_map/reduce_scatter | solution.py:343
  2461.5 828.1 %reduce-scatter.11.cloned.1.call-done = f32[64,12288]{1,0:T(8,128)} async-done(((f32[2048,12288]{1,0:T(8,128)}), f32[64,12288]{1,0:T(8,128)}) %reduce-scatter.11.cloned.1.call-update) | async-done | bytes 3145744 | tf_op jit(solution)/shard_map/reduce_scatter | solution.py:289
  (307 shorter events, 583.6 us)
Async XLA Ops:
  7.2 122.8 %all-gather.5.cloned.1.call-start = ((), (), s32[]{:S(2)}) async-start(), calls=%async_computation.12 | async-start | bytes 17301504 | tf_op jit(solution)/shard_map/all_gather | solution.py:186
  9.5 511.5 %all-gather.7.cloned.1.call-start = ((), (), s32[]{:S(2)}) async-start(), calls=%async_computation.13 | async-start | bytes 8650752 | tf_op jit(solution)/shard_map/all_gather | solution.py:187
  11.4 586.3 %all-gather.9.cloned.1.call-start = ((), (), s32[]{:S(2)}) async-start(), calls=%async_computation.14 | async-start | bytes 51904512 | tf_op jit(solution)/shard_map/all_gather | solution.py:188
  12.8 741.9 %all-gather.11.cloned.1.call-start = ((), (), s32[]{:S(2)}) async-start(), calls=%async_computation.15 | async-start | bytes 25952256 | tf_op jit(solution)/shard_map/all_gather | solution.py:189
  59.2 141.8 %copy-start.43 = (f32[128]{0:T(128)}, f32[128]{0:T(128)S(1)}, u32[]{:S(2)}) copy-start(f32[128]{0:T(128)S(1)} %get-tuple-element.411) | copy-start | bytes 1540
  61.3 143.9 %copy-start.18 = (f32[512,64]{1,0:T(8,128)}, f32[512,64]{1,0:T(8,128)S(1)}, u32[]{:S(2)}) copy-start(f32[512,64]{1,0:T(8,128)S(1)} %get-tuple-element.412) | copy-start | bytes 393220
  61.3 143.9 %copy-start.20 = (f32[512,64]{1,0:T(8,128)}, f32[512,64]{1,0:T(8,128)S(1)}, u32[]{:S(2)}) copy-start(f32[512,64]{1,0:T(8,128)S(1)} %get-tuple-element.413) | copy-start | bytes 393220
  148.8 41.1 %all-to-all-start.1 = ((bf16[1,512,8,128]{3,1,0,2:T(8,128)(2,1)}), bf16[1,512,8,128]{3,1,0,2:T(8,128)(2,1)S(1)}, u32[]{:S(2)}, u32[]{:S(2)}) async-start(bf16[1,512,8,128]{3,1,0,2:T(8,128)(2,1)} %pad_maximum_fusion.8), calls=%async_computation.1 | async-start | bytes 2097152 | tf_op jit(solution)/shard_map/all_to_all | solution.py:235
  189.9 51.8 %all-to-all-start.2 = ((bf16[1,512,8,128]{3,1,0,2:T(8,128)(2,1)}), bf16[1,512,8,128]{3,1,0,2:T(8,128)(2,1)S(1)}, u32[]{:S(2)}, u32[]{:S(2)}) async-start(bf16[1,512,8,128]{3,1,0,2:T(8,128)(2,1)} %copy.294), calls=%async_computation.2 | async-start | bytes 2097152 | tf_op jit(solution)/shard_map/all_to_all | solution.py:242
  242.7 85.8 %all-to-all-start = ((bf16[1,512,16,128]{3,1,0,2:T(8,128)(2,1)}), bf16[1,512,16,128]{3,1,0,2:T(8,128)(2,1)S(1)}, u32[]{:S(2)}, u32[]{:S(2)}) async-start(bf16[1,512,16,128]{3,1,0,2:T(8,128)(2,1)} %maximum_bitcast_fusion), calls=%async_computation | async-start | bytes 4194304 | tf_op jit(solution)/shard_map/all_to_all | solution.py:228
  246.3 1399.1 %reduce-scatter.9.cloned.1.call-start = ((), (), s32[]{:S(2)}) async-start(), calls=%async_computation.17 | async-start | bytes 17301504 | tf_op jit(solution)/shard_map/reduce_scatter | solution.py:344
  406.1 109.0 %copy-start.2 = (bf16[2048,2,128]{2,0,1:T(8,128)(2,1)}, bf16[2048,2,128]{2,0,1:T(8,128)(2,1)S(1)}, u32[]{:S(2)}) copy-start(bf16[2048,2,128]{2,0,1:T(8,128)(2,1)S(1)} %get-tuple-element.618) | copy-start | bytes 3145732
  406.1 109.0 %copy-start.11 = (bf16[2048,2,2,128]{3,0,2,1:T(8,128)(2,1)}, bf16[2048,2,2,128]{3,0,2,1:T(8,128)(2,1)S(1)}, u32[]{:S(2)}) copy-start(bf16[2048,2,2,128]{3,0,2,1:T(8,128)(2,1)S(1)} %get-tuple-element.623) | copy-start | bytes 6291460
  531.7 291.6 %copy-start.27 = (f32[512]{0:T(512)}, f32[512]{0:T(512)S(1)}, u32[]{:S(2)}) copy-start(f32[512]{0:T(512)S(1)} %add_rsqrt_fusion.2) | copy-start | bytes 6148
  839.2 904.7 %reduce-scatter.13.cloned.1.call-start = ((), (), s32[]{:S(2)}) async-start(), calls=%async_computation.19 | async-start | bytes 51904512 | tf_op jit(solution)/shard_map/reduce_scatter | solution.py:290
  924.2 107.8 %all-to-all-start.4 = ((bf16[1,512,16,128]{3,1,0,2:T(8,128)(2,1)}), bf16[1,512,16,128]{3,1,0,2:T(8,128)(2,1)}, u32[]{:S(2)}, u32[]{:S(2)}) async-start(bf16[1,512,16,128]{3,1,0,2:T(8,128)(2,1)} %copy.301), calls=%async_computation.4 | async-start | bytes 4194304 | tf_op jit(solution)/shard_map/all_to_all | solution.py:299
  928.7 108.1 %copy-start.3 = (bf16[2048,2,128]{2,0,1:T(8,128)(2,1)S(1)}, bf16[2048,2,128]{2,0,1:T(8,128)(2,1)}, u32[]{:S(2)}) copy-start(bf16[2048,2,128]{2,0,1:T(8,128)(2,1)} %copy-done.2) | copy-start | bytes 3145732
  1290.5 30.0 all-to-all-start.6
  1320.5 57.8 %all-to-all-start.7 = ((bf16[1,2048,2,128]{3,2,0,1:T(2,128)(2,1)}), bf16[1,2048,2,128]{3,2,0,1:T(2,128)(2,1)}, u32[]{:S(2)}, u32[]{:S(2)}) async-start(bf16[1,2048,2,128]{3,2,0,1:T(2,128)(2,1)} %bitcast.338), calls=%async_computation.7 | async-start | bytes 2097152 | tf_op jit(solution)/shard_map/all_to_all | solution.py:311
  1378.2 100.0 %all-to-all-start.5 = ((bf16[1,2048,4,128]{3,2,0,1:T(4,128)(2,1)}), bf16[1,2048,4,128]{3,2,0,1:T(4,128)(2,1)S(1)}, u32[]{:S(2)}, u32[]{:S(2)}) async-start(bf16[1,2048,4,128]{3,2,0,1:T(4,128)(2,1)} %copy.304), calls=%async_computation.5 | async-start | bytes 4194304 | tf_op jit(solution)/shard_map/all_to_all | solution.py:305
  1381.8 1075.3 %reduce-scatter.7.cloned.1.call-start = ((), (), s32[]{:S(2)}) async-start(), calls=%async_computation.16 | async-start | bytes 34603008 | tf_op jit(solution)/shard_map/reduce_scatter | solution.py:343
  1513.2 1776.4 %reduce-scatter.11.cloned.1.call-start = ((), (), s32[]{:S(2)}) async-start(), calls=%async_computation.18 | async-start | bytes 103809024 | tf_op jit(solution)/shard_map/reduce_scatter | solution.py:289
  1645.5 98.5 %copy-start.22 = (f32[64,6144]{1,0:T(8,128)S(1)}, f32[64,6144]{1,0:T(8,128)}, u32[]{:S(2)}) copy-start(f32[64,6144]{1,0:T(8,128)} %param.28) | copy-start | bytes 4718596
  1749.2 1540.4 %copy-start.10 = (f32[64,12288]{1,0:T(8,128)S(1)}, f32[64,12288]{1,0:T(8,128)}, u32[]{:S(2)}) copy-start(f32[64,12288]{1,0:T(8,128)} %param.27) | copy-start | bytes 9437188
  (49 other events, 1103.8 us)
Sparse Core Ops, SparseCore 0:
  11.6 118.3 all-gather.4
  133.5 109.9 all-gather.6
  247.0 350.5 all-gather.8
  600.9 153.6 all-gather.10
  839.3 399.0 reduce-scatter.8
  1244.7 499.1 reduce-scatter.12
  1746.2 710.8 reduce-scatter.6
  2463.6 825.9 reduce-scatter.10
where the time goes:
time: 3310 us; the launch traced here: 3300 us
  waiting for transfers between devices  2280 us (69%)
  matrix products  480 us (15%)
  blocking collectives  190 us (6%)
  other arithmetic  170 us (5%)
  local copies, waits for them, and re-layouts  132 us (4%)
    reduce_scatter x1, waiting for transfers between devices, whole_plan(): lax.psum_scatter(sum_gate_up, ('dp', 'seq'), scatter_dimension=0, tiled=T...  828 us
    reduce_scatter x1, waiting for transfers between devices, whole_plan(): lax.psum_scatter(sum_in, ('dp', 'seq'), scatter_dimension=0, tiled=True)  708 us
    all_gather x1, waiting for transfers between devices, gather_whole(): lax.all_gather(down_part, ('dp', 'seq'), axis=0, tiled=True)  120 us
    all_to_all x1, blocking collectives, whole_plan(): lax.all_to_all(attended.astype(jnp.bfloat16), 'seq', split_axis=1, concat...  105 us
    all_to_all x1, waiting for transfers between devices, whole_plan(): lax.all_to_all(grad_attended, 'seq', split_axis=2, concat_axis=1, tiled=T...  103 us
    reduce_scatter x1, waiting for transfers between devices, whole_plan(): lax.psum_scatter(sum_down, ('dp', 'seq'), scatter_dimension=0, tiled=True)  95.8 us
    dot_general x4, matrix products, contract_rows(): lax.dot_general(left, right, (((0,), (0,)), ((), ())), preferred_element_...  93 us
    unnamed x2, blocking collectives  84.9 us
  transfers between devices with their start and end apart: 15, of which 13 were waited for; matrix products, arithmetic and copies ran while one was open for 20% of the time, Pallas kernels for 0%

commit v1 on v0

v1 whole, which is shorter than its diff:
```python
import functools
import math
import jax
import jax.numpy as jnp
from jax import lax
from jax.sharding import Mesh
from jax.sharding import PartitionSpec as P
from jax.experimental import pallas as pl
from jax.experimental.pallas import tpu as pltpu

HEAD_SIZE = 128
REPEATS = 2
SLOTS = 4
norm_eps = 1e-06
masked_score = -1e30
MIB = 1024 * 1024
LOG2E = 1.4426950408889634


def params(mib):
    return pltpu.CompilerParams(vmem_limit_bytes=mib * MIB)


def dot(left, right, left_dim, right_dim):
    return lax.dot_general(
        left, right, (((left_dim,), (right_dim,)), ((), ())), preferred_element_type=jnp.float32
    )


def head(slot):
    return slice(slot * HEAD_SIZE, (slot + 1) * HEAD_SIZE)


def rotary_forward_kernel(query_ref, key_ref, value_ref, cos_ref, sin_ref, gain_ref, out_ref):
    cosine, sine = cos_ref[...], sin_ref[...]
    for slot in range(REPEATS + 1):
        values = query_ref[:, head(slot)] if slot < REPEATS else key_ref[...]
        _, values = normed_rows(values)
        values = values * gain_ref[slot][None, :]
        values = values * cosine + pltpu.roll(values, HEAD_SIZE // 2, 1) * sine
        out_ref[0, :, head(slot)] = values.astype(jnp.bfloat16)
    out_ref[0, :, head(REPEATS + 1)] = value_ref[...].astype(jnp.bfloat16)


def rotary_forward(raw, cosine, sine, gain_heads, part, count):
    rows, width = raw.shape
    tokens, wide = rows // 2, SLOTS * HEAD_SIZE
    every = width // wide
    groups = every // count
    start = part * groups
    return pl.pallas_call(
        rotary_forward_kernel,
        grid=(2, groups),
        in_specs=[
            pl.BlockSpec((tokens, REPEATS * HEAD_SIZE), lambda s, g: (s, start + g)),
            pl.BlockSpec((tokens, HEAD_SIZE), lambda s, g: (s, every * REPEATS + start + g)),
            pl.BlockSpec((tokens, HEAD_SIZE), lambda s, g: (s, every * (REPEATS + 1) + start + g)),
            pl.BlockSpec((tokens, HEAD_SIZE), lambda s, g: (s, 0)),
            pl.BlockSpec((tokens, HEAD_SIZE), lambda s, g: (s, 0)),
            pl.BlockSpec(gain_heads.shape, lambda s, g: (0, 0)),
        ],
        out_specs=pl.BlockSpec((1, tokens, wide), lambda s, g: (s * groups + g, 0, 0)),
        out_shape=jax.ShapeDtypeStruct((2 * groups, tokens, wide), jnp.bfloat16),
        compiler_params=params(24),
        cost_estimate=pl.CostEstimate(flops=0, bytes_accessed=rows * width, transcendentals=0),
        name="rotary_forward",
    )(raw, raw, raw, cosine, sine, gain_heads)


def rotary_backward_kernel(count, *refs):
    grad_refs = refs[:count]
    raw_ref, cos_ref, sin_ref, gain_ref, out_ref, sum_ref = refs[count:]
    groups = grad_refs[0].shape[0]

    @pl.when(pl.program_id(0) == 0)
    def _():
        sum_ref[...] = jnp.zeros_like(sum_ref)

    cosine, sine = cos_ref[...], sin_ref[...]
    every = count * groups
    for part in range(count):
        for group in range(groups):
            for slot in range(SLOTS):
                grad = grad_refs[part][group, :, head(slot)]
                at = part * groups + group
                columns = head(at * REPEATS + slot if slot < REPEATS else every * slot + at)
                if slot <= REPEATS:
                    grad = grad.astype(jnp.float32)
                    grad = grad * cosine - pltpu.roll(grad, HEAD_SIZE // 2, 1) * sine
                    values = raw_ref[:, columns]
                    scale, normed = normed_rows(values)
                    product = grad * normed
                    sum_ref[slot, :] += jnp.sum(product, axis=0)
                    gain = gain_ref[slot][None, :]
                    inner = jnp.mean(product * gain, axis=-1, keepdims=True)
                    grad = (scale * (grad * gain - normed * inner)).astype(jnp.bfloat16)
                out_ref[:, columns] = grad


def rotary_backward(grads, raw, cosine, sine, gain_heads):
    rows, width = raw.shape
    groups, tokens, wide = grads[0].shape
    block = min(256, tokens)
    steps = tokens // block
    table = pl.BlockSpec((block, HEAD_SIZE), lambda i: (i, 0))
    return pl.pallas_call(
        functools.partial(rotary_backward_kernel, len(grads)),
        grid=(2 * steps,),
        in_specs=[
            pl.BlockSpec((groups // 2, block, wide), lambda i: (i // steps, i % steps, 0))
            for _ in grads
        ]
        + [
            pl.BlockSpec((block, width), lambda i: (i, 0)),
            table,
            table,
            pl.BlockSpec(gain_heads.shape, lambda i: (0, 0)),
        ],
        out_specs=[
            pl.BlockSpec((block, width), lambda i: (i, 0)),
            pl.BlockSpec((8, HEAD_SIZE), lambda i: (0, 0)),
        ],
        out_shape=[
            jax.ShapeDtypeStruct((rows, width), jnp.bfloat16),
            jax.ShapeDtypeStruct((8, HEAD_SIZE), jnp.float32),
        ],
        compiler_params=params(32),
        cost_estimate=pl.CostEstimate(flops=0, bytes_accessed=rows * width, transcendentals=0),
        name="rotary_backward",
    )(*grads, raw, cosine, sine, gain_heads)


def to_columns_kernel(*refs):
    out_ref = refs[-1]
    width = refs[0].shape[2]
    at = 0
    for ref in refs[:-1]:
        for group in range(ref.shape[0]):
            out_ref[:, at : at + width] = ref[group]
            at += width


def to_columns(parts):
    groups, tokens, width = parts[0].shape
    wide = len(parts) * groups // 2 * width
    return pl.pallas_call(
        to_columns_kernel,
        grid=(2,),
        in_specs=[pl.BlockSpec((groups // 2, tokens, width), lambda s: (s, 0, 0)) for _ in parts],
        out_specs=pl.BlockSpec((tokens, wide), lambda s: (s, 0)),
        out_shape=jax.ShapeDtypeStruct((2 * tokens, wide), parts[0].dtype),
        compiler_params=params(16),
        cost_estimate=pl.CostEstimate(flops=0, bytes_accessed=tokens * wide, transcendentals=0),
        name="to_columns",
    )(*parts)


def from_columns_kernel(values_ref, *out_refs):
    width = out_refs[0].shape[2]
    at = 0
    for ref in out_refs:
        for group in range(ref.shape[0]):
            ref[group] = values_ref[:, at : at + width]
            at += width


def from_columns(values, count, groups):
    rows, wide = values.shape
    tokens, width = rows // 2, wide // (count * groups)
    return pl.pallas_call(
        from_columns_kernel,
        grid=(2,),
        in_specs=[pl.BlockSpec((tokens, wide), lambda s: (s, 0))],
        out_specs=[pl.BlockSpec((groups, tokens, width), lambda s: (s, 0, 0))] * count,
        out_shape=[jax.ShapeDtypeStruct((2 * groups, tokens, width), values.dtype)] * count,
        compiler_params=params(16),
        cost_estimate=pl.CostEstimate(flops=0, bytes_accessed=tokens * wide, transcendentals=0),
        name="from_columns",
    )(values)


def causal_mask(scores):
    keys = lax.broadcasted_iota(jnp.int32, scores.shape, 0)
    queries = lax.broadcasted_iota(jnp.int32, scores.shape, 1)
    return keys <= queries


def attend_kernel(query_ref, other_ref, out_ref, sums_ref):
    block = pl.program_id(1)
    scaling = HEAD_SIZE ** (-0.5) * LOG2E

    def step(index, carry, diagonal):
        keys = other_ref[index, 0, :, head(0)]
        values = other_ref[index, 0, :, head(1)]
        result = []
        for repeat in range(REPEATS):
            queries = query_ref[0, 0, :, head(repeat)]
            scores = dot(keys, queries, 1, 1) * scaling
            if diagonal:
                scores = jnp.where(causal_mask(scores), scores, masked_score)
            highest = jnp.max(scores, axis=0, keepdims=True)
            if not diagonal:
                old_highest, old_total, old_sums = carry[repeat]
                highest = jnp.maximum(highest, old_highest)
            weights = jnp.exp2(scores - highest)
            total = jnp.sum(weights, axis=0, keepdims=True)
            sums = dot(values, weights.astype(jnp.bfloat16), 0, 0)
            if not diagonal:
                rescale = jnp.exp2(old_highest - highest)
                total = total + old_total * rescale
                sums = sums + old_sums * rescale
            result.append((highest, total, sums))
        return tuple(result)

    carry = step(block, None, True)
    carry = lax.fori_loop(0, block, lambda index, now: step(index, now, False), carry)
    for repeat in range(REPEATS):
        highest, total, sums = carry[repeat]
        out_ref[0, 0, :, head(repeat)] = (sums / total).T.astype(jnp.bfloat16)
        sums_ref[0, 0, repeat, :] = (highest + jnp.log2(total))[0]


def attend(parts):
    blocks, units, tokens, _ = parts.shape
    wide = REPEATS * HEAD_SIZE
    return pl.pallas_call(
        attend_kernel,
        grid=(units, blocks),
        in_specs=[
            pl.BlockSpec((1, 1, tokens, wide), lambda u, i: (i, u, 0, 0)),
            pl.BlockSpec((blocks, 1, tokens, wide), lambda u, i: (0, u, 0, 1)),
        ],
        out_specs=[
            pl.BlockSpec((1, 1, tokens, wide), lambda u, i: (i, u, 0, 0)),
            pl.BlockSpec((1, 1, REPEATS, tokens), lambda u, i: (u, i, 0, 0)),
        ],
        out_shape=[
            jax.ShapeDtypeStruct((blocks, units, tokens, wide), jnp.bfloat16),
            jax.ShapeDtypeStruct((units, blocks, REPEATS, tokens), jnp.float32),
        ],
        compiler_params=params(32),
        cost_estimate=pl.CostEstimate(flops=0, bytes_accessed=parts.size, transcendentals=0),
        name="attend",
    )(parts, parts)


def attend_back_kernel(parts_ref, up_ref, attended_ref, sums_ref, out_ref, query_acc, key_acc, value_acc, inner_ref):
    blocks, tokens = parts_ref.shape[0], parts_ref.shape[2]
    scaling = HEAD_SIZE ** (-0.5)
    query_acc[...] = jnp.zeros_like(query_acc)

    def inners(index, _):
        for repeat in range(REPEATS):
            product = up_ref[index, 0, :, head(repeat)].astype(jnp.float32) * attended_ref[
                index, 0, :, head(repeat)
            ].astype(jnp.float32)
            inner_ref[index, repeat, :] = jnp.sum(product.T, axis=0)
        return 0

    lax.fori_loop(0, blocks, inners, 0)

    def pair(key_block, query_block, diagonal):
        keys = parts_ref[key_block, 0, :, head(REPEATS)]
        values = parts_ref[key_block, 0, :, head(REPEATS + 1)]
        for repeat in range(REPEATS):
            queries = parts_ref[query_block, 0, :, head(repeat)]
            upstream = up_ref[query_block, 0, :, head(repeat)]
            scores = dot(keys, queries, 1, 1) * (scaling * LOG2E)
            probs = jnp.exp2(scores - sums_ref[0, query_block, repeat, :][None, :])
            if diagonal:
                probs = jnp.where(causal_mask(probs), probs, 0.0)
            grads = dot(values, upstream, 1, 1)
            grads = (probs * (grads - inner_ref[query_block, repeat, :][None, :])).astype(
                jnp.bfloat16
            )
            value_acc[...] += dot(probs.astype(jnp.bfloat16), upstream, 1, 0)
            key_acc[...] += dot(grads, queries, 1, 0)
            query_acc[query_block, :, head(repeat)] += dot(grads, keys, 0, 0)

    def column(key_block, _):
        key_acc[...] = jnp.zeros_like(key_acc)
        value_acc[...] = jnp.zeros_like(value_acc)
        pair(key_block, key_block, True)

        def later(query_block, _):
            pair(key_block, query_block, False)
            return 0

        lax.fori_loop(key_block + 1, blocks, later, 0)
        out_ref[key_block, 0, :, head(REPEATS)] = (key_acc[...] * scaling).astype(jnp.bfloat16)
        out_ref[key_block, 0, :, head(REPEATS + 1)] = value_acc[...].astype(jnp.bfloat16)
        return 0

    lax.fori_loop(0, blocks, column, 0)
    out_ref[:, 0, :, : REPEATS * HEAD_SIZE] = (query_acc[...] * scaling).astype(jnp.bfloat16)


def attend_back(parts, upstream, attended, log_sums):
    blocks, units, tokens, wide = parts.shape
    half = REPEATS * HEAD_SIZE
    whole = pl.BlockSpec((blocks, 1, tokens, wide), lambda u: (0, u, 0, 0))
    part = pl.BlockSpec((blocks, 1, tokens, half), lambda u: (0, u, 0, 0))
    return pl.pallas_call(
        attend_back_kernel,
        grid=(units,),
        in_specs=[
            whole,
            part,
            part,
            pl.BlockSpec((1, blocks, REPEATS, tokens), lambda u: (u, 0, 0, 0)),
        ],
        out_specs=whole,
        out_shape=jax.ShapeDtypeStruct(parts.shape, jnp.bfloat16),
        scratch_shapes=[
            pltpu.VMEM((blocks, tokens, half), jnp.float32),
            pltpu.VMEM((tokens, HEAD_SIZE), jnp.float32),
            pltpu.VMEM((tokens, HEAD_SIZE), jnp.float32),
            pltpu.VMEM((blocks, REPEATS, tokens), jnp.float32),
        ],
        compiler_params=params(44),
        cost_estimate=pl.CostEstimate(
            flops=0,
            bytes_accessed=parts.size,
            transcendentals=0,
        ),
        name="attend_back",
    )(parts, upstream, attended, log_sums)


def mixed_tiles(values):
    low_half = lax.broadcasted_iota(jnp.int32, (values.shape[0], HEAD_SIZE), 1) < HEAD_SIZE // 2
    tiles = [values[:, head(at)] for at in range(values.shape[1] // HEAD_SIZE)]
    rolled = [pltpu.roll(tile, HEAD_SIZE // 2, 1) for tile in tiles]
    result = []
    for at in range(0, len(tiles), 4):
        for upper, lower in ((at, at + 2), (at + 1, at + 3)):
            result.append(jnp.where(low_half, tiles[upper], rolled[lower]))
            result.append(jnp.where(low_half, rolled[upper], tiles[lower]))
    return jnp.concatenate(result, axis=1)


def unmixed_tiles(values):
    low_half = lax.broadcasted_iota(jnp.int32, (values.shape[0], HEAD_SIZE), 1) < HEAD_SIZE // 2
    tiles = [values[:, head(at)] for at in range(values.shape[1] // HEAD_SIZE)]
    rolled = [pltpu.roll(tile, HEAD_SIZE // 2, 1) for tile in tiles]
    result = []
    for at in range(0, len(tiles), 4):
        upper = [jnp.where(low_half, tiles[at + k], rolled[at + k + 1]) for k in (0, 2)]
        lower = [jnp.where(low_half, rolled[at + k], tiles[at + k + 1]) for k in (0, 2)]
        result += upper + lower
    return jnp.concatenate(result, axis=1)


def loaded(ref, mixed):
    values = ref[...].astype(jnp.float32)
    return mixed_tiles(values) if mixed else values


def normed_rows(values):
    scale = lax.rsqrt(jnp.mean(values * values, axis=-1, keepdims=True) + norm_eps)
    return scale, values * scale


def back_rows(values, gradient, gain):
    scale, normed = normed_rows(values)
    product = gradient * normed
    inner = jnp.mean(product * gain, axis=-1, keepdims=True)
    return scale * (gradient * gain - normed * inner), jnp.sum(product, axis=0, keepdims=True)


def prepare_kernel(mixed, hidden_ref, up_ref, gain_ref, out_ref, up_out_ref):
    _, normed = normed_rows(loaded(hidden_ref, mixed))
    out_ref[...] = (normed * gain_ref[...]).astype(jnp.bfloat16)
    up_out_ref[...] = loaded(up_ref, mixed).astype(jnp.bfloat16)


def middle_kernel(mixed, hidden_ref, own_ref, other_ref, gain_ref, residual_ref, out_ref):
    residual = loaded(hidden_ref, mixed) + (own_ref[...] + other_ref[...].astype(jnp.float32))
    residual_ref[...] = residual
    _, normed = normed_rows(residual)
    out_ref[...] = (normed * gain_ref[...]).astype(jnp.bfloat16)


def outgoing_kernel(mixed, residual_ref, own_ref, other_ref, out_ref):
    result = residual_ref[...] + (own_ref[...] + other_ref[...].astype(jnp.float32))
    if mixed:
        result = unmixed_tiles(result)
    out_ref[...] = result.astype(jnp.bfloat16)


def middle_back_kernel(
    own_ref, other_ref, residual_ref, up_ref, gain_ref, grad_ref, low_ref, sum_ref
):
    @pl.when(pl.program_id(0) == 0)
    def _():
        sum_ref[...] = jnp.zeros_like(sum_ref)

    gradient = own_ref[...] + other_ref[...].astype(jnp.float32)
    back, sums = back_rows(residual_ref[...], gradient, gain_ref[...])
    sum_ref[...] += sums
    back = up_ref[...].astype(jnp.float32) + back
    grad_ref[...] = back
    low_ref[...] = back.astype(jnp.bfloat16)


def incoming_back_kernel(
    mixed, own_ref, other_ref, hidden_ref, later_ref, gain_ref, grad_ref, sum_ref
):
    @pl.when(pl.program_id(0) == 0)
    def _():
        sum_ref[...] = jnp.zeros_like(sum_ref)

    gradient = own_ref[...] + other_ref[...].astype(jnp.float32)
    back, sums = back_rows(loaded(hidden_ref, mixed), gradient, gain_ref[...])
    sum_ref[...] += sums
    back = later_ref[...] + back
    grad_ref[...] = unmixed_tiles(back) if mixed else back


def row_kernel(kernel, operands, results):
    rows, width = operands[0].shape
    block = min(128, rows)

    def spec(shape):
        if shape[0] == 1:
            return pl.BlockSpec((1, width), lambda i: (0, 0))
        return pl.BlockSpec((block, width), lambda i: (i, 0))

    return pl.pallas_call(
        kernel,
        grid=(rows // block,),
        in_specs=[spec(operand.shape) for operand in operands],
        out_specs=[spec((count, width)) for count, _ in results],
        out_shape=[jax.ShapeDtypeStruct((count, width), kind) for count, kind in results],
        compiler_params=params(40),
        cost_estimate=pl.CostEstimate(flops=0, bytes_accessed=rows * width, transcendentals=0),
        name="rows",
    )(*operands)


def sums_kernel(place_ref, left_ref, right_ref, *refs):
    total = dot(left_ref[...], right_ref[...], 1, 0)
    for ref in refs[:-1]:
        total = total + ref[...].astype(jnp.float32)
    refs[-1][...] = total.astype(jnp.bfloat16)


def column_tile(width):
    return 512 if width % 512 == 0 else width


def block_sums(places, left, right, half, *added):
    rows, depth = left.shape
    block, width = rows // 4, right.shape[1] // 2
    count = places.shape[0]
    tile = column_tile(width)
    steps = width // tile
    return pl.pallas_call(
        sums_kernel,
        grid_spec=pltpu.PrefetchScalarGridSpec(
            num_scalar_prefetch=1,
            grid=(count, steps),
            in_specs=[
                pl.BlockSpec((block, depth), lambda i, j, at: (at[i], 0)),
                pl.BlockSpec((depth, tile), lambda i, j, at: (0, half * steps + j)),
            ]
            + [
                pl.BlockSpec((block, tile), functools.partial(lambda which, i, j, at: (which, j), which))
                for _, which in added
            ],
            out_specs=pl.BlockSpec((block, tile), lambda i, j, at: (i, j)),
        ),
        out_shape=jax.ShapeDtypeStruct((count * block, width), jnp.bfloat16),
        compiler_params=params(24),
        cost_estimate=pl.CostEstimate(flops=0, bytes_accessed=block * width, transcendentals=0),
        name="block_sums",
    )(places, left, right, *(array for array, _ in added))


def own_sums_kernel(steps, place_ref, left_ref, right_ref, *refs):
    out_ref = refs[-1]
    total = dot(left_ref[...], right_ref[...], 1, 0)
    first = refs[0][...].astype(jnp.float32) + refs[1][...].astype(jnp.float32)
    second = refs[2][...].astype(jnp.float32) + refs[3][...].astype(jnp.float32)
    total = total + jnp.where(pl.program_id(0) < steps, first, second)
    out_ref[...] = total.astype(jnp.bfloat16)


def own_sums(place, left, right, first, second):
    rows, depth = left.shape
    block, width = rows // 4, right.shape[1] // 2
    tile = column_tile(width)
    steps = width // tile

    def part(which, column):
        return pl.BlockSpec((block, tile), lambda j, at: (which, column(j)))

    return pl.pallas_call(
        functools.partial(own_sums_kernel, steps),
        grid_spec=pltpu.PrefetchScalarGridSpec(
            num_scalar_prefetch=1,
            grid=(2 * steps,),
            in_specs=[
                pl.BlockSpec((block, depth), lambda j, at: (at[0], 0)),
                pl.BlockSpec((depth, tile), lambda j, at: (0, j)),
            ]
            + [part(which, lambda j: jnp.minimum(j, steps - 1)) for _, which in first]
            + [part(which, lambda j: jnp.maximum(j - steps, 0)) for _, which in second],
            out_specs=pl.BlockSpec((block, tile), lambda j, at: (0, j)),
        ),
        out_shape=jax.ShapeDtypeStruct((block, 2 * width), jnp.bfloat16),
        compiler_params=params(24),
        cost_estimate=pl.CostEstimate(flops=0, bytes_accessed=block * width, transcendentals=0),
        name="own_sums",
    )(place, left, right, *(array for array, _ in (*first, *second)))


def partial_kernel(count, *refs):
    own_ref, other_ref = refs[-2:]
    total = dot(refs[0][...], refs[count][...], 1, 1)
    for at in range(1, count):
        total = total + dot(refs[at][...], refs[count + at][...], 1, 1)
    rows = own_ref.shape[0]
    own_ref[...] = total[:rows]
    other_ref[...] = total[rows:].astype(jnp.bfloat16)


def partial_sums(values, weights):
    rows, width = values[0].shape[0], weights[0].shape[0]
    tile = 256
    halves = pl.BlockSpec((rows // 2, tile), lambda j: (0, j))
    return pl.pallas_call(
        functools.partial(partial_kernel, len(values)),
        grid=(width // tile,),
        in_specs=[pl.BlockSpec(value.shape, lambda j: (0, 0)) for value in values]
        + [pl.BlockSpec((tile, weight.shape[1]), lambda j: (j, 0)) for weight in weights],
        out_specs=[halves, halves],
        out_shape=[
            jax.ShapeDtypeStruct((rows // 2, width), jnp.float32),
            jax.ShapeDtypeStruct((rows // 2, width), jnp.bfloat16),
        ],
        compiler_params=params(48),
        cost_estimate=pl.CostEstimate(flops=0, bytes_accessed=rows * width, transcendentals=0),
        name="partial_sums",
    )(*values, *weights)


MODEL_WIDTH = 2048
QUERY_HEADS = 16
KEY_VALUE_HEADS = 8
FF = 6144
STEP = 10

rope_base = 1000000.0
beta_one = 0.9
beta_two = 0.95
adam_eps = 1e-08
weight_decay = 0.1

CORES = 2
COLUMNS = 2
EVERY = ("row", "col", "core", "seq")


def rotary_tables(places):
    half_dim = HEAD_SIZE // 2
    freqs = jnp.exp(
        jnp.arange(half_dim, dtype=jnp.float32) * (-2.0 * math.log(rope_base) / HEAD_SIZE)
    )
    angles = places.astype(jnp.float32)[:, None] * freqs[None, :]
    cosine, sine = jnp.cos(angles), jnp.sin(angles)
    return (
        jnp.concatenate([cosine, cosine], axis=1),
        jnp.concatenate([-sine, sine], axis=1),
    )


def contract_rows(left, right):
    return dot(left, right, 0, 0)


def times(left, right):
    return dot(left, right, 1, 0)


def times_transposed(left, right):
    return dot(left, right, 1, 1)


def low(values):
    return values.astype(jnp.bfloat16)


def full(values):
    return values.astype(jnp.float32)


def shift(values, axis, distance):
    size = lax.axis_size(axis)
    return lax.ppermute(values, axis, [(at, (at + distance) % size) for at in range(size)])


def after(values, *earlier):
    if not earlier:
        return values
    return lax.optimization_barrier((values,) + earlier)[0]


def both_cores(values):
    return jnp.concatenate([values, shift(values, "core", 1)], axis=0)


def own_pair(part, core, spans):
    def half(which):
        pieces = [
            low(lax.dynamic_slice_in_dim(part, start + which * (width // 2), width // 2, 1))
            for start, width in spans
        ]
        return pieces[0] if len(pieces) == 1 else jnp.concatenate(pieces, axis=1)

    kept, received = half(core), shift(half(1 - core), "core", 1)
    return jnp.concatenate(
        [jnp.where(core == 0, kept, received), jnp.where(core == 0, received, kept)], axis=0
    )


def own_rows(pair, core, spans):
    rows = pair.shape[0] // 2
    top, bottom = low(pair[:rows]), low(pair[rows:])
    kept = jnp.where(core == 0, top, bottom)
    received = shift(jnp.where(core == 0, bottom, top), "core", 1)
    halves = jnp.where(core == 0, kept, received), jnp.where(core == 0, received, kept)
    pieces, at = [], 0
    for _, width in spans:
        pieces += [half[:, at : at + width // 2] for half in halves]
        at += width // 2
    return full(jnp.concatenate(pieces, axis=1))


class Plan:
    def __init__(self):
        self.sent, self.arrived, self.pending, self.before = [], [], [], []

    def send(self, values, axis, pairs=((0, 1), (1, 0))):
        result = lax.ppermute(after(values, *self.arrived), axis, pairs)
        self.sent.append(result)
        return result

    def close(self, *also):
        if self.sent or also:
            self.arrived = self.pending = self.sent + list(also)
        self.sent = []

    def now(self, value):
        return after(value, *self.arrived)

    def wait(self, value):
        value = after(value, *self.before, *self.pending)
        self.pending = []
        return value

    def step(self, work, value):
        result = work(self.wait(value))
        self.before = [result]
        return result


def linked():
    return tuple(lax.axis_size(axis) for axis in ("row", "col", "seq")) == (2, 2, 4)


class Gather:
    def __init__(self, plan, pair):
        self.plan, self.pair, self.linked = plan, pair, linked()
        self.parts = []

    def a(self):
        if self.linked:
            other = self.plan.send(self.pair, "seq", ((0, 1), (1, 0), (2, 3), (3, 2)))
            even = lax.axis_index("seq") % 2 == 0
            self.near = jnp.concatenate(
                [jnp.where(even, self.pair, other), jnp.where(even, other, self.pair)], axis=0
            )
            self.parts.append((0, 0, 0, self.near))

    def b(self):
        if self.linked:
            self.middle = self.plan.send(self.near, "seq", ((1, 2), (2, 1)))

    def c(self):
        if self.linked:
            outer = self.plan.send(self.middle, "seq", ((1, 0), (2, 3)))
            seq = lax.axis_index("seq")
            self.far = jnp.where((seq == 1) | (seq == 2), self.middle, outer)
            self.parts.append((0, 0, 1, self.far))

    def near_x(self):
        if self.linked:
            self.near_across = self.plan.send(self.near, "col")
            self.parts.append((0, 1, 0, self.near_across))

    def near_y(self):
        if self.linked:
            self.parts.append((1, 0, 0, self.plan.send(self.near, "row")))

    def near_xy(self):
        if self.linked:
            self.parts.append((1, 1, 0, self.plan.send(self.near_across, "row")))

    def far_x(self):
        if self.linked:
            self.parts.append((0, 1, 1, self.plan.send(self.far, "col")))

    def far_y(self):
        if self.linked:
            self.far_below = self.plan.send(self.far, "row")
            self.parts.append((1, 0, 1, self.far_below))

    def far_yx(self):
        if self.linked:
            self.parts.append((1, 1, 1, self.plan.send(self.far_below, "col")))

    def whole(self, *earlier):
        if not self.linked:
            return lax.all_gather(self.pair, ("row", "col", "seq"), axis=0, tiled=True)
        places = tuple(part[:3] for part in self.parts)
        operands = [part[3] for part in self.parts]
        operands = lax.optimization_barrier((*operands, *earlier))[: len(operands)]
        height, width = self.near.shape
        shape = (height * len(operands), width)
        anywhere = pl.BlockSpec(memory_space=pl.ANY)
        return pl.pallas_call(
            functools.partial(assemble_kernel, places),
            in_specs=[anywhere] * len(operands),
            out_specs=anywhere,
            out_shape=jax.ShapeDtypeStruct(shape, jnp.bfloat16),
            scratch_shapes=[
                pltpu.VMEM(shape, jnp.bfloat16),
                pltpu.SemaphoreType.DMA((len(places),)),
                pltpu.SemaphoreType.DMA((len(places),)),
            ],
            compiler_params=params(shape[0] * shape[1] * 2 // MIB + 4),
            cost_estimate=pl.CostEstimate(
                flops=0, bytes_accessed=shape[0] * shape[1], transcendentals=0
            ),
            name="assemble",
        )(*operands)


def assemble_kernel(places, *refs):
    out_ref, staging, load_sems, store_sems = refs[-4:]
    row, col, seq = lax.axis_index("row"), lax.axis_index("col"), lax.axis_index("seq")
    loads, stores = [], []
    for number, (down, across, other) in enumerate(places):
        height = refs[number].shape[0]
        plane = lax.rem(row + down, 2) * 2 + lax.rem(col + across, 2)
        half = lax.rem(lax.div(seq, 2) + other, 2)
        start = pl.multiple_of((plane * 2 + half) * height, height)
        staged = staging.at[pl.ds(number * height, height)]
        loads.append(pltpu.make_async_copy(refs[number], staged, load_sems.at[number]))
        target = out_ref.at[pl.ds(start, height)]
        stores.append(pltpu.make_async_copy(staged, target, store_sems.at[number]))
    for load in loads:
        load.start()
    for load, store in zip(loads, stores):
        load.wait()
        store.start()
    for store in stores:
        store.wait()


class Scatter:
    def __init__(self, plan, left, right):
        self.plan, self.left, self.right, self.linked = plan, left, right, linked()

    def sums(self, half, *places_and_added):
        places = [step for step in places_and_added if not hasattr(step[0], "dtype")]
        added = [step for step in places_and_added if hasattr(step[0], "dtype")]
        row, col = lax.axis_index("row"), lax.axis_index("col")
        where = jnp.stack([(row + down) % 2 * 2 + (col + across) % 2 for down, across in places])
        return self.plan.step(
            lambda value: block_sums(value, self.left, self.right, half, *added),
            where.astype(jnp.int32),
        )

    def prepare(self):
        if self.linked:
            self.to_send = self.sums(0, (1, 1), (0, 1)), self.sums(1, (1, 1), (1, 0))

    def crossing(self):
        if self.linked:
            self.to_cross = self.sums(0, (1, 1)), self.sums(1, (1, 1))

    def straight(self):
        if self.linked:
            self.to_go = self.sums(0, (0, 1)), self.sums(1, (1, 0))

    def send(self):
        if self.linked:
            came = self.plan.send(self.to_send[0], "col"), self.plan.send(self.to_send[1], "row")
            self.crossed = [(part, 0) for part in came]
            self.straight = [(part, 1) for part in came]

    def send_crossing(self):
        if self.linked:
            came = self.plan.send(self.to_cross[0], "col"), self.plan.send(self.to_cross[1], "row")
            self.crossed = [(part, 0) for part in came]

    def send_straight(self):
        if self.linked:
            came = self.plan.send(self.to_go[0], "col"), self.plan.send(self.to_go[1], "row")
            self.straight = [(part, 0) for part in came]

    def turn(self):
        if self.linked:
            self.to_turn = (
                self.sums(0, (1, 0), self.crossed[0]),
                self.sums(1, (0, 1), self.crossed[1]),
            )

    def send_turned(self):
        if self.linked:
            came = self.plan.send(self.to_turn[0], "row"), self.plan.send(self.to_turn[1], "col")
            self.turned = [(part, 0) for part in came]

    def last(self):
        if not self.linked:
            return low(dot(self.left, self.right, 1, 0))
        first, second = zip(self.straight, self.turned)
        place = (lax.axis_index("row") * 2 + lax.axis_index("col")).astype(jnp.int32)[None]
        return self.plan.step(
            lambda value: own_sums(value, self.left, self.right, first, second), place
        )


def scatter_last(own):
    axes = ("seq",) if linked() else ("row", "col", "seq")
    return lax.psum_scatter(own, axes, scatter_dimension=0, tiled=True)


def adamw_update(param, gradient, first, second, rate, decay):
    first = beta_one * first + (1.0 - beta_one) * gradient
    second = beta_two * second + (1.0 - beta_two) * gradient * gradient
    first_hat = first / (1.0 - beta_one**STEP)
    second_hat = second / (1.0 - beta_two**STEP)
    param = param - rate * (first_hat / (jnp.sqrt(second_hat) + adam_eps) + decay * param)
    return (param, first, second)


def per_device(
    hidden_in,
    positions,
    cotangent,
    input_projection,
    out_proj,
    gate_up,
    down_proj,
    gains,
    input_first_moment,
    input_second_moment,
    out_first,
    out_second,
    gate_first,
    gate_second,
    down_first,
    down_second,
    gain_first,
    gain_second,
):
    core = lax.axis_index("core")
    quads, depth = lax.axis_size("row") * lax.axis_size("col"), lax.axis_size("seq")
    devices = quads * CORES * depth
    _, tokens, width = hidden_in.shape
    rows = width // devices
    groups = KEY_VALUE_HEADS // CORES
    count = 2 * groups // depth
    part_groups = groups // count
    mixed_order = linked() and rows == HEAD_SIZE // CORES

    def to_gathered(values):
        return (
            values.reshape(-1, quads, CORES, depth, rows)
            .transpose(0, 1, 3, 2, 4)
            .reshape(values.shape)
        )

    def from_gathered(values):
        return (
            values.reshape(-1, quads, depth, CORES, rows)
            .transpose(0, 1, 3, 2, 4)
            .reshape(values.shape)
        )

    plan = Plan()
    key_width = KEY_VALUE_HEADS * HEAD_SIZE
    in_spans = (
        (0, REPEATS * key_width),
        (REPEATS * key_width, key_width),
        ((REPEATS + 1) * key_width, key_width),
    )
    gate_span, up_span = (0, FF), (FF, FF)
    out_span, down_span = (0, out_proj.shape[1]), (0, FF)
    in_pair = own_pair(input_projection, core, in_spans)
    in_gather = Gather(plan, in_pair)
    in_gather.a()
    gains_low = lax.all_to_all(
        jnp.broadcast_to(low(gains)[None], (devices, gains.shape[0])),
        EVERY,
        split_axis=0,
        concat_axis=0,
        tiled=True,
    ).reshape(-1)
    plan.close(gains_low)

    in_gather.near_x(), in_gather.near_y(), in_gather.b()
    gate_pair = own_pair(plan.now(gate_up), core, [gate_span])
    gate_gather = Gather(plan, gate_pair)
    out_gather = Gather(plan, own_pair(after(out_proj, gate_pair), core, [out_span]))
    gate_gather.a(), out_gather.a()
    plan.close()

    in_gather.near_xy(), in_gather.c(), gate_gather.b(), gate_gather.near_x()
    plan.close()

    in_gather.far_x(), gate_gather.near_y(), gate_gather.c(), out_gather.b()
    up_pair = own_pair(plan.now(gate_up), core, [up_span])
    up_gather = Gather(plan, up_pair)
    down_pair = own_pair(plan.now(down_proj), core, [down_span])
    down_gather = Gather(plan, down_pair)
    plan.close(up_pair, down_pair)

    gate_gather.far_x(), in_gather.far_y(), up_gather.a(), down_gather.a()
    gain_all = full(gains_low)
    gain_attn = to_gathered(gain_all[:width])[None]
    gain_mlp = to_gathered(gain_all[width : 2 * width])[None]
    gain_query = gain_all[2 * width : 2 * width + HEAD_SIZE]
    gain_key = gain_all[2 * width + HEAD_SIZE :]
    gain_heads = jnp.stack([gain_query] * REPEATS + [gain_key])
    hidden_own, upstream_own = plan.now(hidden_in[0]), cotangent[0]
    if not mixed_order:
        hidden_own, upstream_own = to_gathered(hidden_own), to_gathered(upstream_own)
    attn_own, upstream_own = row_kernel(
        functools.partial(prepare_kernel, mixed_order),
        [hidden_own, upstream_own, gain_attn],
        [(tokens, jnp.bfloat16)] * 2,
    )
    plan.close(attn_own)

    in_gather.far_yx(), gate_gather.far_y(), up_gather.b(), out_gather.c()
    attn_in = both_cores(plan.now(attn_own))
    cosine, sine = rotary_tables(both_cores(positions[0]))
    plan.close(attn_in, cosine, sine)

    def exchange(values):
        return lax.all_to_all(values, "seq", split_axis=0, concat_axis=0, tiled=True)

    def to_heads(values):
        return exchange(values)[:, None]

    def to_tokens(values):
        return exchange(values[:, 0])

    gate_gather.far_yx(), gate_gather.near_xy(), up_gather.c(), down_gather.b()
    in_low = in_gather.whole()
    projected = times(plan.now(attn_in), in_low)
    parts = [
        rotary_forward(projected, cosine, sine, gain_heads, part, count) for part in range(count)
    ]
    plan.close(*parts)

    up_gather.near_x(), up_gather.near_y(), out_gather.near_x(), out_gather.near_y()
    head_parts = [to_heads(plan.now(parts[0]))]
    plan.close(head_parts[0])

    up_gather.far_x(), up_gather.far_y(), out_gather.far_x(), out_gather.far_y()
    attended, log_sums, returned = [], [], []

    def attention(part):
        result, sums = attend(plan.now(head_parts[part]))
        attended.append(result)
        log_sums.append(sums)

    if count == 2:
        head_parts.append(to_heads(plan.now(parts[1])))
    attention(0)
    plan.close(head_parts[-1], attended[0])

    up_gather.far_yx(), up_gather.near_xy(), out_gather.far_yx(), out_gather.near_xy()
    down_gather.c()
    returned.append(to_tokens(plan.now(attended[0])))
    if count == 2:
        attention(1)
    plan.close(attended[-1])

    down_gather.near_x(), down_gather.near_y()
    if count == 2:
        returned.append(to_tokens(plan.now(attended[1])))
    gate_low, up_low = gate_gather.whole(*plan.arrived), up_gather.whole(*plan.arrived)
    upstream = both_cores(plan.now(upstream_own))
    attn_turned, upstream_turned = plan.now(attn_in).T, upstream.T
    plan.close(*returned, gate_low, up_low, upstream)

    down_gather.far_x(), down_gather.far_y()
    mixed = to_columns([plan.now(values) for values in returned])
    out_low = out_gather.whole()
    own, other = partial_sums([mixed], [out_low])
    plan.close(own)

    down_gather.far_yx(), down_gather.near_xy()
    residual, mlp_own = row_kernel(
        functools.partial(middle_kernel, mixed_order),
        [hidden_own, own, shift(plan.now(other), "core", 1), gain_mlp],
        [(tokens, jnp.float32), (tokens, jnp.bfloat16)],
    )
    mlp_low = both_cores(mlp_own)
    gate_pre = times(mlp_low, gate_low)
    up_pre = times(after(mlp_low, gate_pre, attn_turned, upstream_turned), up_low)
    mlp_turned = after(mlp_low, up_pre).T
    down_low = down_gather.whole(up_pre)
    gate_sig = jax.nn.sigmoid(gate_pre)
    gate_act = gate_pre * gate_sig
    hidden = low(gate_act * up_pre)
    grad_hidden = times(upstream, down_low)
    grad_gate = low(grad_hidden * up_pre * gate_sig * (1.0 + gate_pre * (1.0 - gate_sig)))
    grad_up = low(grad_hidden * gate_act)

    plan = Plan()
    down_scatter = Scatter(plan, upstream_turned, hidden)
    gate_scatter = Scatter(plan, mlp_turned, grad_gate)
    up_scatter = Scatter(plan, mlp_turned, grad_up)

    down_scatter.crossing()
    down_scatter.send_crossing()
    down_scatter.straight()
    own, other = partial_sums([plan.wait(grad_gate), grad_up], [gate_low, up_low])
    plan.before = [other]
    plan.close(own)

    down_scatter.send_straight()
    grad_residual, grad_attn_own, sum_g_mlp = row_kernel(
        middle_back_kernel,
        [own, shift(plan.now(other), "core", 1), residual, upstream_own, gain_mlp],
        [(tokens, jnp.float32), (tokens, jnp.bfloat16), (1, jnp.float32)],
    )
    down_scatter.turn()
    gate_scatter.crossing()
    gate_scatter.straight()
    plan.close(grad_attn_own, *plan.before)

    down_scatter.send_turned()
    grad_attn_out = both_cores(plan.now(grad_attn_own))
    grad_attended = low(times(grad_attn_out, out_low))
    plan.close(grad_attended)

    gate_scatter.send_crossing()
    grad_attended = from_columns(grad_attended, count, part_groups)
    grad_heads = [to_heads(grad_attended[0])]
    if count == 2:
        grad_heads.append(to_heads(after(grad_attended[1], grad_heads[0])))
    up_scatter.crossing()
    up_scatter.straight()
    out_scatter = Scatter(plan, grad_attn_out.T, mixed)
    out_scatter.prepare()
    plan.close(*plan.before, grad_heads[0])

    gate_scatter.send_straight()
    grad_parts = []

    def attention_back(part):
        return plan.step(
            lambda value: attend_back(head_parts[part], value, attended[part], log_sums[part]),
            grad_heads[part],
        )

    grad_part = attention_back(0)
    gate_scatter.turn()
    plan.close(*plan.before)

    gate_scatter.send_turned()
    grad_parts.append(to_tokens(grad_part))
    if count == 2:
        grad_part = attention_back(1)
    down_own = down_scatter.last()
    plan.close(*plan.before, grad_parts[0])

    up_scatter.send_crossing()
    out_scatter.send()
    if count == 2:
        grad_parts.append(to_tokens(plan.now(grad_part)))
    mlp_own, mlp_other = partial_sums([plan.wait(hidden)], [down_low])
    plan.before = [mlp_other]
    gate_own = gate_scatter.last()
    plan.close(*plan.before, grad_parts[-1])

    up_scatter.send_straight()
    out_scatter.turn()
    out_scatter.send_turned()
    up_scatter.turn()
    down_sum = scatter_last(plan.now(down_own))
    gate_sum = scatter_last(plan.now(gate_own))
    plan.close(*plan.before)

    up_scatter.send_turned()
    grad_projected, head_gain_sums = rotary_backward(
        [plan.wait(values) for values in grad_parts], projected, cosine, sine, gain_heads
    )
    plan.before = [grad_projected]
    sum_g_query = jnp.sum(head_gain_sums[:REPEATS], axis=0)
    sum_g_key = head_gain_sums[REPEATS]
    in_scatter = Scatter(plan, attn_turned, grad_projected)
    in_scatter.prepare()
    out_own = out_scatter.last()
    plan.close(*plan.before)

    in_scatter.send()
    (layer_out,) = row_kernel(
        functools.partial(outgoing_kernel, mixed_order),
        [residual, mlp_own, shift(plan.now(mlp_other), "core", 1)],
        [(tokens, jnp.bfloat16)],
    )
    up_own = up_scatter.last()
    both_sums = scatter_last(jnp.concatenate([up_own, out_own], axis=1))
    up_sum, out_sum = both_sums[:, : up_own.shape[1]], both_sums[:, up_own.shape[1] :]
    own, other = partial_sums([plan.wait(grad_projected)], [in_low])
    plan.before = [other]
    plan.close(*plan.before, down_sum, gate_sum, layer_out)

    in_scatter.turn()
    in_scatter.send_turned()
    input_grad, sum_g_attn = row_kernel(
        functools.partial(incoming_back_kernel, mixed_order),
        [own, shift(plan.now(other), "core", 1), hidden_own, grad_residual, gain_attn],
        [(tokens, jnp.float32), (1, jnp.float32)],
    )
    sum_gains = jnp.concatenate(
        [from_gathered(sum_g_attn[0]), from_gathered(sum_g_mlp[0]), sum_g_query, sum_g_key]
    )
    gain_grad = jnp.sum(
        lax.all_to_all(
            plan.now(sum_gains).reshape(devices, -1),
            EVERY,
            split_axis=0,
            concat_axis=0,
            tiled=True,
        ),
        axis=0,
    )
    down_grad = own_rows(plan.now(down_sum), core, [down_span])
    plan.close()

    in_sum = scatter_last(after(in_scatter.last(), both_sums))
    if not mixed_order:
        layer_out, input_grad = from_gathered(layer_out), from_gathered(input_grad)

    rate = 1.0 / math.sqrt(MODEL_WIDTH)
    out_rate = 8.0 / math.sqrt(QUERY_HEADS * HEAD_SIZE)
    down_rate = 1.0 / math.sqrt(FF)
    gate_grad = own_rows(
        jnp.concatenate([gate_sum, up_sum], axis=1), core, [gate_span, up_span]
    )
    gate_new = adamw_update(gate_up, gate_grad, gate_first, gate_second, rate, weight_decay)
    down_new = adamw_update(down_proj, down_grad, down_first, down_second, down_rate, weight_decay)
    out_grad = own_rows(out_sum, core, [out_span])
    out_new = adamw_update(out_proj, out_grad, out_first, out_second, out_rate, weight_decay)
    in_grad = own_rows(in_sum, core, in_spans)
    in_new = adamw_update(
        input_projection, in_grad, input_first_moment, input_second_moment, rate, weight_decay
    )
    gain_new = adamw_update(gains, gain_grad, gain_first, gain_second, 0.5, 0.0)
    return (
        layer_out[None],
        input_grad[None],
        *in_new,
        *out_new,
        *gate_new,
        *down_new,
        *gain_new,
    )


def solution(mesh):
    dp, seq = mesh.devices.shape
    chips = Mesh(mesh.devices.reshape(dp // (COLUMNS * CORES), COLUMNS, CORES, seq), EVERY)
    tokens = P(("row", "col", "core"), "seq", None)
    places = P(("row", "col", "core"), "seq")
    weight = P(EVERY, None)
    gain = P(EVERY)
    return jax.shard_map(
        per_device,
        mesh=chips,
        in_specs=(tokens, places, tokens) + (weight,) * 4 + (gain,) + (weight,) * 8 + (gain,) * 2,
        out_specs=(tokens, tokens) + (weight,) * 12 + (gain,) * 3,
        check_vma=False,
    )
```

time: 3310 us -> 1200 us (0.36)
  waiting for transfers between devices: 2280 us -> 432 us
  matrix products: 480 us -> 83.5 us
  Pallas kernels: 0 us -> 303 us
  blocking collectives: 190 us -> 0 us
  other arithmetic: 170 us -> 60.7 us
  starting transfers between devices: 27.5 us -> 135 us
    reduce_scatter x4, waiting for transfers between devices: 1630 us -> 53.5 us  [scatter_last(): return lax.psum_scatter(own, axes, scatter_dimension=0, tiled=True)]
    dot_general x40 -> x5, matrix products: 480 us -> 83.5 us  [dot(): lax.dot_general(left, right, (((left_dim,), (right_dim,)), ((), ())), pre...]
    all_to_all x7 -> x10, waiting for transfers between devices: 390 us -> 15.9 us  [the longest x1 11.3 us: per_device(): lax.all_to_all(jnp.broadcast_to(low(gains)[None], (devices, gains.shape[0...]
    ppermute x0 -> x89, waiting for transfers between devices: none -> 362 us  [the longest x71 351 us: send(): result = lax.ppermute(after(values, *self.arrived), axis, pairs)]
    pallas_call x0 -> x54, Pallas kernels: none -> 303 us  [the longest x26 79 us: block_sums(): pl.pallas_call(sums_kernel, grid_spec=pltpu.PrefetchScalarGridSpec(num_sc...]
    all_gather x4 -> x0, waiting for transfers between devices: 254 us -> none  [the longest x1 120 us: gather_whole(): lax.all_gather(down_part, ('dp', 'seq'), axis=0, tiled=True)]
    all_to_all x1 -> x0, blocking collectives: 105 us -> none  [whole_plan(): lax.all_to_all(attended.astype(jnp.bfloat16), 'seq', split_axis=1, concat...]
    unnamed x2 -> x0, blocking collectives: 84.9 us -> none
  transfers between devices with their start and end apart: 15 -> 103, of which waited for: 13 -> 42; matrix products, arithmetic and copies ran while one was open for 20% -> 11% of each run, Pallas kernels for 0% -> 25%
where the time goes in v1:
time: 1200 us; the launch traced here: 1190 us
  waiting for transfers between devices  432 us (36%)
  Pallas kernels  303 us (25%)
  local copies, waits for them, and re-layouts  156 us (13%)
  starting transfers between devices  135 us (11%)
  matrix products  83.5 us (7%)
  other arithmetic  60.7 us (5%)
  between operations  16.4 us (1%)
    ppermute x71, waiting for transfers between devices, send(): result = lax.ppermute(after(values, *self.arrived), axis, pairs)  351 us
    unnamed x367, local copies, waits for them, and re-layouts  126 us
    dot_general x5, matrix products, dot(): lax.dot_general(left, right, (((left_dim,), (right_dim,)), ((), ())), pre...  83.5 us
    ppermute x71, starting transfers between devices, send(): result = lax.ppermute(after(values, *self.arrived), axis, pairs)  80.7 us
    pallas_call x26, Pallas kernels, block_sums(): pl.pallas_call(sums_kernel, grid_spec=pltpu.PrefetchScalarGridSpec(num_sc...  79 us
    pallas_call x4, Pallas kernels, partial_sums(): pl.pallas_call(functools.partial(partial_kernel, len(values)), grid=(widt...  77.2 us
    reduce_scatter x4, waiting for transfers between devices, scatter_last(): return lax.psum_scatter(own, axes, scatter_dimension=0, tiled=True)  53.5 us
    all_to_all x8, starting transfers between devices, exchange(): lax.all_to_all(values, 'seq', split_axis=0, concat_axis=0, tiled=True)  41.7 us
  transfers between devices with their start and end apart: 103, of which 42 were waited for; matrix products, arithmetic and copies ran while one was open for 11% of the time, Pallas kernels for 25%

profile of v1, /device:TPU:0, one launch (start us, length us, event | category | flops | bytes accessed | tf_op | source)
XLA Modules:
  0.0 1187.7 jit_solution(10854932865397294907)
XLA Ops:
  42.7 13.9 %collective-permute-done.6 = bf16[128,3072]{1,0:T(8,128)(2,1)S(1)} collective-permute-done((bf16[128,3072]{1,0:T(8,128)(2,1)S(1)}, bf16[128,3072]{1,0:T(8,128)(2,1)S(1)}, u32[]{:S(2)}, u32[]{:S(2)}) %collective-permute-start.6) | collective-permute-done | bytes 786464 | tf_op jit(solution)/shard_map/ppermute | solution.py:645
  72.3 23.8 %collective-permute-done.9 = bf16[256,2048]{1,0:T(8,128)(2,1)} collective-permute-done((bf16[256,2048]{1,0:T(8,128)(2,1)}, bf16[256,2048]{1,0:T(8,128)(2,1)}, u32[]{:S(2)}, u32[]{:S(2)}) %collective-permute-start.9) | collective-permute-done | bytes 1048608 | tf_op jit(solution)/shard_map/ppermute | solution.py:645
  114.9 25.7 %collective-permute-done.15 = bf16[256,3072]{1,0:T(8,128)(2,1)S(1)} collective-permute-done((bf16[256,3072]{1,0:T(8,128)(2,1)}, bf16[256,3072]{1,0:T(8,128)(2,1)S(1)}, u32[]{:S(2)}, u32[]{:S(2)}) %collective-permute-start.15) | collective-permute-done | bytes 1572896 | tf_op jit(solution)/shard_map/ppermute | solution.py:645
  169.5 16.7 %collective-permute-done.22 = bf16[128,3072]{1,0:T(8,128)(2,1)} collective-permute-done((bf16[128,3072]{1,0:T(8,128)(2,1)}, bf16[128,3072]{1,0:T(8,128)(2,1)}, u32[]{:S(2)}, u32[]{:S(2)}) %collective-permute-start.22) | collective-permute-done | bytes 786464 | tf_op jit(solution)/shard_map/ppermute | solution.py:645
  200.4 20.9 %collective-permute-done.24.refs_7_ = bf16[256,2048]{1,0:T(8,128)(2,1)S(1)} collective-permute-done((bf16[256,2048]{1,0:T(8,128)(2,1)}, bf16[256,2048]{1,0:T(8,128)(2,1)S(1)}, u32[]{:S(2)}, u32[]{:S(2)}) %collective-permute-start.24) | collective-permute-done | bytes 1048608 | tf_op jit(solution)/shard_map/ppermute | solution.py:645
  252.8 12.3 %collective-permute-done.29.refs_6_ = bf16[256,3072]{1,0:T(8,128)(2,1)S(1)} collective-permute-done((bf16[256,3072]{1,0:T(8,128)(2,1)}, bf16[256,3072]{1,0:T(8,128)(2,1)S(1)}, u32[]{:S(2)}, u32[]{:S(2)}) %collective-permute-start.29) | collective-permute-done | bytes 1572896 | tf_op jit(solution)/shard_map/ppermute | solution.py:645
  280.8 41.5 %collective-permute-done.35.refs_2_ = bf16[256,1024]{1,0:T(8,128)(2,1)S(1)} collective-permute-done((bf16[256,1024]{1,0:T(8,128)(2,1)}, bf16[256,1024]{1,0:T(8,128)(2,1)S(1)}, u32[]{:S(2)}, u32[]{:S(2)}) %collective-permute-start.35) | collective-permute-done | bytes 524320 | tf_op jit(solution)/shard_map/ppermute | solution.py:645
  351.3 26.3 %collective-permute-done.39.refs_4_ = bf16[256,1024]{1,0:T(8,128)(2,1)S(1)} collective-permute-done((bf16[256,1024]{1,0:T(8,128)(2,1)S(1)}, bf16[256,1024]{1,0:T(8,128)(2,1)S(1)}, u32[]{:S(2)}, u32[]{:S(2)}) %collective-permute-start.39) | collective-permute-done | bytes 524320 | tf_op jit(solution)/shard_map/ppermute | solution.py:645
  406.2 17.5 %collective-permute-done.43.refs_6_ = bf16[256,1024]{1,0:T(8,128)(2,1)S(1)} collective-permute-done((bf16[256,1024]{1,0:T(8,128)(2,1)}, bf16[256,1024]{1,0:T(8,128)(2,1)S(1)}, u32[]{:S(2)}, u32[]{:S(2)}) %collective-permute-start.43) | collective-permute-done | bytes 524320 | tf_op jit(solution)/shard_map/ppermute | solution.py:645
  492.4 15.0 %collective-permute-done.49.refs_4_ = bf16[256,3072]{1,0:T(8,128)(2,1)S(1)} collective-permute-done((bf16[256,3072]{1,0:T(8,128)(2,1)}, bf16[256,3072]{1,0:T(8,128)(2,1)S(1)}, u32[]{:S(2)}, u32[]{:S(2)}) %collective-permute-start.49) | collective-permute-done | bytes 1572896 | tf_op jit(solution)/shard_map/ppermute | solution.py:645
  528.1 18.8 %fusion.16 = f32[1024,3072]{1,0:T(8,128)} fusion(bf16[2048,3072]{1,0:T(8,128)(2,1)} %copy-done.32, bf16[512,2048]{0,1:T(8,128)(2,1)} %collective-permute-done.52, bf16[512,2048]{0,1:T(8,128)(2,1)S(1)} %copy.86), kind=kOutput, calls=%fused_computation.135 | convolution fusion | flops 12893290496 | bytes 29360128 | tf_op jit(solution)/shard_map/dot_general | solution.py:25
  549.1 19.8 %fusion.32 = f32[1024,3072]{1,0:T(8,128)} fusion(bf16[1024,2048]{0,1:T(8,128)(2,1)S(1)} %pad_maximum_fusion.2, bf16[2048,3072]{1,0:T(8,128)(2,1)} %copy-done.33), kind=kOutput, calls=%fused_computation.142 | convolution fusion | flops 12884901888 | bytes 29360128 | tf_op jit(solution)/shard_map/dot_general | solution.py:25
  577.1 27.7 %multiply_convert_fusion = (bf16[1024,3072]{1,0:T(8,128)(2,1)}, bf16[1024,3072]{1,0:T(8,128)(2,1)}, bf16[1024,3072]{1,0:T(8,128)(2,1)}) fusion(f32[1024,3072]{1,0:T(8,128)} %fusion.16, f32[1024,3072]{1,0:T(8,128)} %fusion.32, bf16[2048,3072]{1,0:T(8,128)(2,1)} %copy-done.31, bf16[512,2048]{0,1:T(8,128)(2,1)} %collective-permute-done.48, ...), kind=kOutput, calls=%fused_computation | convolution fusion | flops 12940476416 | bytes 60817408 | tf_op jit(solution)/shard_map/dot_general | solution.py:25
  629.3 34.2 %partial_sums.5 = (f32[512,2048]{1,0:T(8,128)}, bf16[512,2048]{1,0:T(8,128)(2,1)S(1)}) custom-call(bf16[1024,3072]{1,0:T(8,128)(2,1)} %get-tuple-element.314.refs_0_.right_ref, bf16[1024,3072]{1,0:T(8,128)(2,1)} %get-tuple-element.416.refs_1_.right_ref, bf16[2048,3072]{1,0:T(8,128)(2,1)} %copy-done.32, bf16[2048,3072]{1,0:T(8,128)(2,1)} %copy-done.33), custom_call_target="tpu_custom_call" | custom-call | bytes 2097152 | tf_op jit(solution)/shard_map/partial_sums/pallas_call | solution.py:532
  724.2 18.9 %collective-permute-done.61.refs_1_ = bf16[512,1536]{1,0:T(8,128)(2,1)} collective-permute-done((bf16[512,1536]{1,0:T(8,128)(2,1)}, bf16[512,1536]{1,0:T(8,128)(2,1)}, u32[]{:S(2)}, u32[]{:S(2)}) %collective-permute-start.61) | collective-permute-done | bytes 1572896 | tf_op jit(solution)/shard_map/ppermute | solution.py:645
  782.5 16.8 %attend_back.2 = bf16[4,1,512,512]{3,2,1,0:T(8,128)(2,1)S(1)} custom-call(bf16[4,1,512,512]{3,2,1,0:T(8,128)(2,1)S(1)} %bitcast.76, bf16[4,1,512,256]{3,2,1,0:T(8,128)(2,1)S(1)} %bitcast.84, bf16[4,1,512,256]{3,2,1,0:T(8,128)(2,1)S(1)} %copy-done.69, f32[1,4,2,512]{3,2,1,0:T(2,128)S(1)} %get-tuple-element.343.sums_ref), custom_call_target="tpu_custom_call" | custom-call | bytes 1048576 | tf_op jit(solution)/shard_map/attend_back/pallas_call | solution.py:303
  825.3 18.1 %attend_back.3 = bf16[4,1,512,512]{3,2,1,0:T(8,128)(2,1)S(1)} custom-call(bf16[4,1,512,512]{3,2,1,0:T(8,128)(2,1)S(1)} %bitcast.73, bf16[4,1,512,256]{3,2,1,0:T(8,128)(2,1)} %bitcast.19.up_ref, bf16[4,1,512,256]{3,2,1,0:T(8,128)(2,1)S(1)} %copy-done.71, f32[1,4,2,512]{3,2,1,0:T(2,128)S(1)} %get-tuple-element.349.sums_ref), custom_call_target="tpu_custom_call" | custom-call | bytes 1048576 | tf_op jit(solution)/shard_map/attend_back/pallas_call | solution.py:303
  865.9 18.8 %partial_sums.6 = (f32[512,2048]{1,0:T(8,128)}, bf16[512,2048]{1,0:T(8,128)(2,1)}) custom-call(bf16[1024,3072]{1,0:T(8,128)(2,1)} %get-tuple-element.353.right_ref.refs_0_, bf16[2048,3072]{1,0:T(8,128)(2,1)} %copy-done.31), custom_call_target="tpu_custom_call" | custom-call | bytes 2097152 | tf_op jit(solution)/shard_map/partial_sums/pallas_call | solution.py:532
  896.9 20.9 %collective-permute-done.71.refs_0_ = bf16[1024,512]{1,0:T(8,128)(2,1)} collective-permute-done((bf16[1024,512]{1,0:T(8,128)(2,1)}, bf16[1024,512]{1,0:T(8,128)(2,1)}, u32[]{:S(2)}, u32[]{:S(2)}) %collective-permute-start.71) | collective-permute-done | bytes 1048608 | tf_op jit(solution)/shard_map/ppermute | solution.py:645
  941.9 24.1 %collective-permute-done.75.refs_1_ = bf16[512,512]{1,0:T(8,128)(2,1)S(1)} collective-permute-done((bf16[512,512]{1,0:T(8,128)(2,1)S(1)}, bf16[512,512]{1,0:T(8,128)(2,1)S(1)}, u32[]{:S(2)}, u32[]{:S(2)}) %collective-permute-start.75) | collective-permute-done | bytes 524320 | tf_op jit(solution)/shard_map/ppermute | solution.py:645
  1008.7 14.4 %partial_sums.7 = (f32[512,2048]{1,0:T(8,128)}, bf16[512,2048]{1,0:T(8,128)(2,1)S(1)}) custom-call(bf16[1024,2048]{1,0:T(8,128)(2,1)} %copy-done.25, bf16[2048,2048]{1,0:T(8,128)(2,1)} %copy-done.39), custom_call_target="tpu_custom_call" | custom-call | bytes 2097152 | tf_op jit(solution)/shard_map/partial_sums/pallas_call | solution.py:532
  1027.9 27.6 %collective-permute-done.80.refs_0_ = bf16[1024,1024]{1,0:T(8,128)(2,1)S(1)} collective-permute-done((bf16[1024,1024]{1,0:T(8,128)(2,1)}, bf16[1024,1024]{1,0:T(8,128)(2,1)S(1)}, u32[]{:S(2)}, u32[]{:S(2)}) %collective-permute-start.80) | collective-permute-done | bytes 2097184 | tf_op jit(solution)/shard_map/ppermute | solution.py:645
  1109.3 12.7 %reduce-scatter.9.cloned.1.call-done = bf16[128,4096]{1,0:T(8,128)(2,1)} async-done(((bf16[512,4096]{1,0:T(8,128)(2,1)}), bf16[128,4096]{1,0:T(8,128)(2,1)}) %reduce-scatter.9.cloned.1.call-update) | async-done | bytes 1048592 | tf_op jit(solution)/shard_map/reduce_scatter | solution.py:838
  1128.3 40.8 %reduce-scatter.11.cloned.1.call-done = bf16[128,2048]{1,0:T(8,128)(2,1)} async-done(((bf16[512,2048]{1,0:T(8,128)(2,1)}), bf16[128,2048]{1,0:T(8,128)(2,1)}) %reduce-scatter.11.cloned.1.call-update) | async-done | bytes 524304 | tf_op jit(solution)/shard_map/reduce_scatter | solution.py:838
  (707 shorter events, 644.0 us)
Async XLA Ops:
  270.7 55.1 %all-to-all-start.1 = ((bf16[4,512,512]{2,1,0:T(8,128)(2,1)}), bf16[4,512,512]{2,1,0:T(8,128)(2,1)S(1)}, u32[]{:S(2)}, u32[]{:S(2)}) async-start(bf16[4,512,512]{2,1,0:T(8,128)(2,1)} %copy-done.49), calls=%async_computation.1 | async-start | bytes 4194304 | tf_op jit(solution)/shard_map/all_to_all | solution.py:955
  276.7 46.8 %collective-permute-start.33 = (bf16[256,3072]{1,0:T(8,128)(2,1)}, bf16[256,3072]{1,0:T(8,128)(2,1)S(1)}, u32[]{:S(2)}, u32[]{:S(2)}) collective-permute-start(bf16[256,3072]{1,0:T(8,128)(2,1)} %copy-done.63), channel_id=1, source_target_pairs={{0,8},{8,0},{1,9},{9,1},{2,10},{10,2},{3,11},{11,3},{4,12},{12,4},... | collective-permute-start | bytes 4718600 | tf_op jit(solution)/shard_map/ppermute | solution.py:645
  277.4 47.2 %collective-permute-start.34 = (bf16[256,3072]{1,0:T(8,128)(2,1)}, bf16[256,3072]{1,0:T(8,128)(2,1)S(1)}, u32[]{:S(2)}, u32[]{:S(2)}) collective-permute-start(bf16[256,3072]{1,0:T(8,128)(2,1)} %copy-done.63), channel_id=1, source_target_pairs={{0,16},{16,0},{1,17},{17,1},{2,18},{18,2},{3,19},{19,3},{4,20},{20... | collective-permute-start | bytes 4718600 | tf_op jit(solution)/shard_map/ppermute | solution.py:645
  327.1 53.5 %all-to-all-start.2 = ((bf16[4,512,512]{2,1,0:T(8,128)(2,1)}), bf16[4,512,512]{2,1,0:T(8,128)(2,1)S(1)}, u32[]{:S(2)}, u32[]{:S(2)}) async-start(bf16[4,512,512]{2,1,0:T(8,128)(2,1)} %copy-done.48), calls=%async_computation.2 | async-start | bytes 4194304 | tf_op jit(solution)/shard_map/all_to_all | solution.py:955
  335.3 45.2 %collective-permute-start.38 = (bf16[256,3072]{1,0:T(8,128)(2,1)S(1)}, bf16[256,3072]{1,0:T(8,128)(2,1)}, u32[]{:S(2)}, u32[]{:S(2)}) collective-permute-start(bf16[256,3072]{1,0:T(8,128)(2,1)S(1)} %broadcast_select_fusion.1.refs_1_), channel_id=1, source_target_pairs={{0,16},{16,0},{1,17},{17,1},{2,18},{18,2},{3,19},{19,3},{4,20},{20... | collective-permute-start | bytes 4718600 | tf_op jit(solution)/shard_map/ppermute | solution.py:645
  382.6 47.5 %collective-permute-start.45 = (bf16[256,3072]{1,0:T(8,128)(2,1)}, bf16[256,3072]{1,0:T(8,128)(2,1)}, u32[]{:S(2)}, u32[]{:S(2)}) collective-permute-start(bf16[256,3072]{1,0:T(8,128)(2,1)} %collective-permute-done.32), channel_id=1, source_target_pairs={{1,0},{2,3},{5,4},{6,7},{9,8},{10,11},{13,12},{14,15},{17,16},{18,... | collective-permute-start | bytes 4718600 | tf_op jit(solution)/shard_map/ppermute | solution.py:645
  383.9 52.0 %all-to-all-start.3 = ((bf16[4,512,256]{2,1,0:T(8,128)(2,1)}), bf16[4,512,256]{2,1,0:T(8,128)(2,1)}, u32[]{:S(2)}, u32[]{:S(2)}) async-start(bf16[4,512,256]{2,1,0:T(8,128)(2,1)} %bitcast.82), calls=%async_computation.3 | async-start | bytes 2097152 | tf_op jit(solution)/shard_map/all_to_all | solution.py:955
  612.3 52.5 %collective-permute-start.55 = (bf16[512,1536]{1,0:T(8,128)(2,1)S(1)}, bf16[512,1536]{1,0:T(8,128)(2,1)}, u32[]{:S(2)}, u32[]{:S(2)}) collective-permute-start(bf16[512,1536]{1,0:T(8,128)(2,1)S(1)} %block_sums.26), channel_id=1, source_target_pairs={{0,8},{8,0},{1,9},{9,1},{2,10},{10,2},{3,11},{11,3},{4,12},{12,4},... | collective-permute-start | bytes 4718600 | tf_op jit(solution)/shard_map/ppermute | solution.py:645
  616.8 48.0 %collective-permute-start.56 = (bf16[512,1536]{1,0:T(8,128)(2,1)}, bf16[512,1536]{1,0:T(8,128)(2,1)}, u32[]{:S(2)}, u32[]{:S(2)}) collective-permute-start(bf16[512,1536]{1,0:T(8,128)(2,1)} %block_sums.27), channel_id=1, source_target_pairs={{0,16},{16,0},{1,17},{17,1},{2,18},{18,2},{3,19},{19,3},{4,20},{20... | collective-permute-start | bytes 4718600 | tf_op jit(solution)/shard_map/ppermute | solution.py:645
  750.2 50.4 %all-to-all-start.6 = ((bf16[4,512,256]{2,1,0:T(8,128)(2,1)}), bf16[4,512,256]{2,1,0:T(8,128)(2,1)}, u32[]{:S(2)}, u32[]{:S(2)}) async-start(bf16[4,512,256]{2,1,0:T(8,128)(2,1)} %get-tuple-element.331), calls=%async_computation.6 | async-start | bytes 2097152 | tf_op jit(solution)/shard_map/all_to_all | solution.py:955
  800.6 56.1 %all-to-all-start.7 = ((bf16[4,512,512]{2,1,0:T(8,128)(2,1)}), bf16[4,512,512]{2,1,0:T(8,128)(2,1)}, u32[]{:S(2)}, u32[]{:S(2)}) async-start(bf16[4,512,512]{2,1,0:T(8,128)(2,1)} %bitcast.81), calls=%async_computation.7 | async-start | bytes 4194304 | tf_op jit(solution)/shard_map/all_to_all | solution.py:955
  856.7 61.6 %all-to-all-start.8 = ((bf16[4,512,512]{2,1,0:T(8,128)(2,1)}), bf16[4,512,512]{2,1,0:T(8,128)(2,1)}, u32[]{:S(2)}, u32[]{:S(2)}) async-start(bf16[4,512,512]{2,1,0:T(8,128)(2,1)} %bitcast.80), calls=%async_computation.8 | async-start | bytes 4194304 | tf_op jit(solution)/shard_map/all_to_all | solution.py:955
  861.8 195.4 %reduce-scatter.5.cloned.1.call-start = ((), (), s32[]{:S(2)}) async-start(), calls=%async_computation.14 | async-start | bytes 3932160 | tf_op jit(solution)/shard_map/reduce_scatter | solution.py:838
  861.8 56.5 %collective-permute-start.69 = (bf16[512,1536]{1,0:T(8,128)(2,1)}, bf16[512,1536]{1,0:T(8,128)(2,1)}, u32[]{:S(2)}, u32[]{:S(2)}) collective-permute-start(bf16[512,1536]{1,0:T(8,128)(2,1)} %copy-done.106), channel_id=1, source_target_pairs={{0,8},{8,0},{1,9},{9,1},{2,10},{10,2},{3,11},{11,3},{4,12},{12,4},... | collective-permute-start | bytes 4718600 | tf_op jit(solution)/shard_map/ppermute | solution.py:645
  862.6 55.7 %collective-permute-start.70 = (bf16[512,1536]{1,0:T(8,128)(2,1)}, bf16[512,1536]{1,0:T(8,128)(2,1)}, u32[]{:S(2)}, u32[]{:S(2)}) collective-permute-start(bf16[512,1536]{1,0:T(8,128)(2,1)} %copy-done.105), channel_id=1, source_target_pairs={{0,16},{16,0},{1,17},{17,1},{2,18},{18,2},{3,19},{19,3},{4,20},{20... | collective-permute-start | bytes 4718600 | tf_op jit(solution)/shard_map/ppermute | solution.py:645
  863.3 54.5 %collective-permute-start.71 = (bf16[1024,512]{1,0:T(8,128)(2,1)}, bf16[1024,512]{1,0:T(8,128)(2,1)}, u32[]{:S(2)}, u32[]{:S(2)}) collective-permute-start(bf16[1024,512]{1,0:T(8,128)(2,1)} %copy-done.120), channel_id=1, source_target_pairs={{0,8},{8,0},{1,9},{9,1},{2,10},{10,2},{3,11},{11,3},{4,12},{12,4},... | collective-permute-start | bytes 3145736 | tf_op jit(solution)/shard_map/ppermute | solution.py:645
  864.6 53.7 %collective-permute-start.72 = (bf16[1024,512]{1,0:T(8,128)(2,1)}, bf16[1024,512]{1,0:T(8,128)(2,1)}, u32[]{:S(2)}, u32[]{:S(2)}) collective-permute-start(bf16[1024,512]{1,0:T(8,128)(2,1)} %copy-done.119), channel_id=1, source_target_pairs={{0,16},{16,0},{1,17},{17,1},{2,18},{18,2},{3,19},{19,3},{4,20},{20... | collective-permute-start | bytes 3145736 | tf_op jit(solution)/shard_map/ppermute | solution.py:645
  918.3 139.0 %reduce-scatter.7.cloned.1.call-start = ((), (), s32[]{:S(2)}) async-start(), calls=%async_computation.15 | async-start | bytes 3932160 | tf_op jit(solution)/shard_map/reduce_scatter | solution.py:838
  919.1 202.9 %reduce-scatter.9.cloned.1.call-start = ((), (), s32[]{:S(2)}) async-start(), calls=%async_computation.16 | async-start | bytes 5242880 | tf_op jit(solution)/shard_map/reduce_scatter | solution.py:838
  919.1 47.0 %collective-permute-start.73 = (bf16[512,1536]{1,0:T(8,128)(2,1)}, bf16[512,1536]{1,0:T(8,128)(2,1)S(1)}, u32[]{:S(2)}, u32[]{:S(2)}) collective-permute-start(bf16[512,1536]{1,0:T(8,128)(2,1)} %copy-done.92), channel_id=1, source_target_pairs={{0,8},{8,0},{1,9},{9,1},{2,10},{10,2},{3,11},{11,3},{4,12},{12,4},... | collective-permute-start | bytes 4718600 | tf_op jit(solution)/shard_map/ppermute | solution.py:645
  920.5 45.6 %collective-permute-start.74 = (bf16[512,1536]{1,0:T(8,128)(2,1)}, bf16[512,1536]{1,0:T(8,128)(2,1)S(1)}, u32[]{:S(2)}, u32[]{:S(2)}) collective-permute-start(bf16[512,1536]{1,0:T(8,128)(2,1)} %copy-done.91), channel_id=1, source_target_pairs={{0,16},{16,0},{1,17},{17,1},{2,18},{18,2},{3,19},{19,3},{4,20},{20... | collective-permute-start | bytes 4718600 | tf_op jit(solution)/shard_map/ppermute | solution.py:645
  1007.2 48.3 %collective-permute-start.80 = (bf16[1024,1024]{1,0:T(8,128)(2,1)}, bf16[1024,1024]{1,0:T(8,128)(2,1)S(1)}, u32[]{:S(2)}, u32[]{:S(2)}) collective-permute-start(bf16[1024,1024]{1,0:T(8,128)(2,1)} %copy-done.85), channel_id=1, source_target_pairs={{0,8},{8,0},{1,9},{9,1},{2,10},{10,2},{3,11},{11,3},{4,12},{12,4},... | collective-permute-start | bytes 6291464 | tf_op jit(solution)/shard_map/ppermute | solution.py:645
  1008.0 47.9 %collective-permute-start.81 = (bf16[1024,1024]{1,0:T(8,128)(2,1)}, bf16[1024,1024]{1,0:T(8,128)(2,1)S(1)}, u32[]{:S(2)}, u32[]{:S(2)}) collective-permute-start(bf16[1024,1024]{1,0:T(8,128)(2,1)} %copy-done.84), channel_id=1, source_target_pairs={{0,16},{16,0},{1,17},{17,1},{2,18},{18,2},{3,19},{19,3},{4,20},{20... | collective-permute-start | bytes 6291464 | tf_op jit(solution)/shard_map/ppermute | solution.py:645
  1093.9 75.2 %reduce-scatter.11.cloned.1.call-start = ((), (), s32[]{:S(2)}) async-start(), calls=%async_computation.17 | async-start | bytes 2621440 | tf_op jit(solution)/shard_map/reduce_scatter | solution.py:838
  (260 other events, 3684.4 us)
Sparse Core Ops, SparseCore 0:
  918.4 60.6 reduce-scatter.4
  982.0 60.2 reduce-scatter.6
  1044.6 77.3 reduce-scatter.8
  1124.8 44.3 reduce-scatter.10
